TPU v7x, 768 devices: a whole 4x8x12 slice. The times are simulated.
768 devices in a mesh: ax: 12 (over z), cr: 64 (over y, x, core).
Axes of the slice: x: 4, y: 8, z: 12, core: 2. Of those that a mesh axis runs over, the one named last changes fastest.
Arguments:
- parcels: bfloat16 [12, 64, 64, 16, 64], P('ax', 'cr'), may hold values from -6 to 6
- cell_index: int32 [12, 64, 64, 64], P('ax', 'cr'), may hold values from 0 to 131071
- counts: int32 [12, 64, 64], P('ax', 'cr'), may hold values from 0 to 64, as said below
- coupling: bfloat16 [4, 16], replicated, may hold values from -1.5 to 1.5
Outputs:
- smoothed: float32 [4, 384, 2048, 128], P(None, 'ax', 'cr')
Inputs may be any that keep to these rules, and one draw needn't show every extreme that they name: The live slots of a bucket are its first counts[a, c, d]; in every draw some brick receives 64 live parcels from each brick of its slab.
All inputs are finite; a program needn't handle non-finite values.
Results may differ from a plain program's by a relative error of at most 0.0029.
Values may be sent and summed in bfloat16 or wider, within the bound.
A program may use at most 32 MiB of HBM per device.

v0:
```python
import math

import jax
import jax.numpy as jnp
from jax import lax
from jax.sharding import PartitionSpec as P

CA = 32
CY = 32
NZ = 128
COMP = 4
HALF = 16


volume_inv = 256.0
sigma_ratio = 0.75


def padded_2(cells, sides, width):
    for axis, dim in sides:
        count = lax.axis_size(axis)
        ends = count - 1
        head = lax.slice_in_dim(cells, 0, width, axis=dim)
        tail = lax.slice_in_dim(cells, cells.shape[dim] - width, cells.shape[dim], axis=dim)
        cells = jnp.concatenate(
            [
                lax.ppermute(tail, axis, [(i, (i + 1) % count) for i in range(ends)]),
                cells,
                lax.ppermute(head, axis, [((i + 1) % count, i) for i in range(ends)]),
            ],
            axis=dim,
        )
    return cells


def band_matrix(count_out, count_in, first_out, first_in, extent):
    sigma = sigma_ratio * HALF
    out_pos = first_out + jnp.arange(count_out, dtype=jnp.int32)
    in_pos = first_in + jnp.arange(count_in, dtype=jnp.int32)
    spacing = in_pos[None, :] - out_pos[:, None]
    spacing_f = spacing.astype(jnp.float32)
    kernel = jnp.where(
        jnp.abs(spacing) <= HALF, jnp.exp(-spacing_f * spacing_f / (2.0 * sigma * sigma)), 0.0
    )
    offsets = jnp.arange(-HALF, HALF + 1, dtype=jnp.int32)
    offsets_f = offsets.astype(jnp.float32)
    tap_values = jnp.exp(-offsets_f * offsets_f / (2.0 * sigma * sigma))
    reach = out_pos[:, None] + offsets[None, :]
    inside = (reach >= 0) & (reach < extent)
    weight_sum = jnp.sum(jnp.where(inside, tap_values[None, :], 0.0), axis=1)
    return kernel / weight_sum[:, None]


def on_device(parcels, cell_index, counts, coupling):
    bricks = lax.axis_size("cr")
    capacity = parcels.shape[-1]
    slot_ids = jnp.arange(capacity, dtype=jnp.int32)
    live_mask = slot_ids[None, :] < counts[0, 0][:, None]
    kept = jnp.where(live_mask[:, None, :], parcels[0, 0], jnp.zeros((), jnp.bfloat16))
    arrived, places = (
        lax.all_to_all(kept[None, None], "cr", split_axis=2, concat_axis=1, tiled=True),
        lax.all_to_all(cell_index, "cr", split_axis=2, concat_axis=1, tiled=True),
    )
    sources = jnp.einsum(
        "fj,sjk->sfk", coupling, arrived[0, :, 0], preferred_element_type=jnp.float32
    )
    sources = sources.astype(jnp.bfloat16)
    places = places[0, :, 0]
    per_block = math.gcd(bricks, max(1, 512 // capacity))
    block_count = bricks // per_block
    block_rows = per_block * capacity
    source_blocks = sources.reshape(block_count, per_block, COMP, capacity)
    source_blocks = source_blocks.transpose(0, 2, 1, 3).reshape(block_count, COMP, block_rows)
    place_blocks = places.reshape(block_count, block_rows)
    plane_ids = jnp.arange(CA * CY, dtype=jnp.int32)
    depth_ids = jnp.arange(NZ, dtype=jnp.int32)

    def add_block(running, block_data):
        block_sources, block_places = block_data
        plane_of = block_places // NZ
        depth_of = block_places % NZ
        pick_plane = (plane_ids[:, None] == plane_of[None, :]).astype(jnp.bfloat16)
        pick_depth = (depth_of[:, None] == depth_ids[None, :]).astype(jnp.bfloat16)
        weighted = block_sources[:, :, None] * pick_depth[None, :, :]
        running = running + jnp.einsum(
            "pr,frz->fpz", pick_plane, weighted, preferred_element_type=jnp.float32
        )
        return (running, None)

    start_fields = jnp.zeros((COMP, CA * CY, NZ), jnp.float32)
    fields, _ = lax.scan(add_block, start_fields, (source_blocks, place_blocks))
    fields = fields.reshape(COMP, CA, CY, NZ)
    band_depth = band_matrix(NZ, NZ, 0, 0, NZ)
    fields = jnp.einsum(
        "fayz,wz->fayw",
        fields,
        band_depth,
        precision=lax.Precision.HIGHEST,
        preferred_element_type=jnp.float32,
    )
    axial_first = lax.axis_index("ax") * CA
    cross_first = lax.axis_index("cr") * CY
    band_axial = band_matrix(
        CA, CA + 2 * HALF, axial_first, axial_first - HALF, CA * lax.axis_size("ax")
    )
    band_cross = band_matrix(CY, CY + 2 * HALF, cross_first, cross_first - HALF, CY * bricks)
    padded = padded_2(fields, (("ax", 1),), HALF)
    fields = jnp.einsum(
        "fayz,ba->fbyz",
        padded,
        band_axial,
        precision=lax.Precision.HIGHEST,
        preferred_element_type=jnp.float32,
    )
    padded = padded_2(fields, (("cr", 2),), HALF)
    fields = jnp.einsum(
        "fayz,cy->facz",
        padded,
        band_cross,
        precision=lax.Precision.HIGHEST,
        preferred_element_type=jnp.float32,
    )
    return volume_inv * fields


def solution(mesh):
    return jax.shard_map(
        on_device,
        mesh=mesh,
        in_specs=(
            P("ax", "cr", None, None, None),
            P("ax", "cr", None, None),
            P("ax", "cr", None),
            P(),
        ),
        out_specs=P(None, "ax", "cr", None),
        check_vma=False,
    )
```

profile of v0, /device:TPU:520, one launch (start us, length us, event | category | flops | bytes accessed | tf_op | source)
XLA Modules:
  0.0 120.9 jit_solution(12426473092217824617)
XLA Ops:
  0.0 10.7 %all-to-all-start.1 = ((s32[1,1,64,64]{3,1,0,2:T(1,128)}), s32[1,1,64,64]{3,1,0,2:T(1,128)S(1)}, u32[]{:S(2)}, u32[]{:S(2)}) async-start(s32[1,1,64,64]{3,1,0,2:T(1,128)} %bitcast.73), calls=%async_computation.1 | async-start | bytes 65536 | tf_op jit(solution)/shard_map/all_to_all | solution.py:62
  10.7 0.7 iota_compare_fusion.2
  11.4 1.0 fusion.88
  12.5 0.9 reshape.130
  13.3 6.0 %all-to-all-done.1 = s32[1,1,64,64]{3,1,0,2:T(1,128)S(1)} async-done(((s32[1,1,64,64]{3,1,0,2:T(1,128)}), s32[1,1,64,64]{3,1,0,2:T(1,128)S(1)}, u32[]{:S(2)}, u32[]{:S(2)}) %all-to-all-start.1) | async-done | bytes 16416 | tf_op jit(solution)/shard_map/all_to_all | solution.py:62
  19.3 5.5 %all-to-all-start = ((bf16[64,2,512]{2,1,0:T(2,128)(2,1)}), bf16[64,2,512]{2,1,0:T(2,128)(2,1)S(1)}, u32[]{:S(2)}, u32[]{:S(2)}) async-start(bf16[64,2,512]{2,1,0:T(2,128)(2,1)} %reshape.130), calls=%async_computation | async-start | bytes 262144 | tf_op jit(solution)/shard_map/all_to_all | solution.py:61
  26.2 8.9 %all-to-all-done = bf16[64,2,512]{2,1,0:T(2,128)(2,1)S(1)} async-done(((bf16[64,2,512]{2,1,0:T(2,128)(2,1)}), bf16[64,2,512]{2,1,0:T(2,128)(2,1)S(1)}, u32[]{:S(2)}, u32[]{:S(2)}) %all-to-all-start) | async-done | bytes 131104 | tf_op jit(solution)/shard_map/all_to_all | solution.py:61
  35.7 10.8 %while.13 = (s32[]{:T(128)}, f32[4,1024,128]{1,2,0:T(8,128)S(1)}, bf16[8,4,512]{2,1,0:T(4,128)(2,1)S(1)}, s32[8,512]{1,0:T(8,128)S(1)}, s32[]{:T(128)}, /*index=5*/s32[]{:T(128)}) while((s32[]{:T(128)}, f32[4,1024,128]{1,2,0:T(8,128)S(1)}, bf16[8,4,512]{2,1,0:T(4,128)(2,1)S(1)}, s32[8,512]{1,0:T(8,128)S(1)}, s32[]{:T(128)}, ...), condition=%wide.region_3.4_spmd.clone, body=%wide.region_2.3_spmd.clone.sunk | while | flops 538850304 | bytes 4483167 | solution.py:91
  35.8 1.2 %bitcast_add_fusion.2 = f32[4,1024,128]{1,2,0:T(8,128)S(1)} fusion(f32[4,1024,128]{1,2,0:T(8,128)S(1)} %get-tuple-element.159, s32[512]{0:T(512)S(1)} %bitcast.71, pred[]{:T(512)S(6)} %compare.12, bf16[512,128]{0,1:T(8,128)(2,1)S(1)} %fusion.95, bf16[4,512]{1,0:T(4,128)(2,1)S(1)} %dynamic-slice_bitcast_fusion.2), kind=kOutput, calls=%fused_computation.2.clone.1 | convolution fusion | flops 538705920 | bytes 4331521 | tf_op jit(solution)/shard_map/while/body/eval_jaxpr/pr,frz->fpz/dot_general | solution.py:85
  37.2 1.2 %bitcast_add_fusion.2 = f32[4,1024,128]{1,2,0:T(8,128)S(1)} fusion(f32[4,1024,128]{1,2,0:T(8,128)S(1)} %get-tuple-element.159, s32[512]{0:T(512)S(1)} %bitcast.71, pred[]{:T(512)S(6)} %compare.12, bf16[512,128]{0,1:T(8,128)(2,1)S(1)} %fusion.95, bf16[4,512]{1,0:T(4,128)(2,1)S(1)} %dynamic-slice_bitcast_fusion.2), kind=kOutput, calls=%fused_computation.2.clone.1 | convolution fusion | flops 538705920 | bytes 4331521 | tf_op jit(solution)/shard_map/while/body/eval_jaxpr/pr,frz->fpz/dot_general | solution.py:85
  38.5 1.2 %bitcast_add_fusion.2 = f32[4,1024,128]{1,2,0:T(8,128)S(1)} fusion(f32[4,1024,128]{1,2,0:T(8,128)S(1)} %get-tuple-element.159, s32[512]{0:T(512)S(1)} %bitcast.71, pred[]{:T(512)S(6)} %compare.12, bf16[512,128]{0,1:T(8,128)(2,1)S(1)} %fusion.95, bf16[4,512]{1,0:T(4,128)(2,1)S(1)} %dynamic-slice_bitcast_fusion.2), kind=kOutput, calls=%fused_computation.2.clone.1 | convolution fusion | flops 538705920 | bytes 4331521 | tf_op jit(solution)/shard_map/while/body/eval_jaxpr/pr,frz->fpz/dot_general | solution.py:85
  39.8 1.2 %bitcast_add_fusion.2 = f32[4,1024,128]{1,2,0:T(8,128)S(1)} fusion(f32[4,1024,128]{1,2,0:T(8,128)S(1)} %get-tuple-element.159, s32[512]{0:T(512)S(1)} %bitcast.71, pred[]{:T(512)S(6)} %compare.12, bf16[512,128]{0,1:T(8,128)(2,1)S(1)} %fusion.95, bf16[4,512]{1,0:T(4,128)(2,1)S(1)} %dynamic-slice_bitcast_fusion.2), kind=kOutput, calls=%fused_computation.2.clone.1 | convolution fusion | flops 538705920 | bytes 4331521 | tf_op jit(solution)/shard_map/while/body/eval_jaxpr/pr,frz->fpz/dot_general | solution.py:85
  41.2 1.2 %bitcast_add_fusion.2 = f32[4,1024,128]{1,2,0:T(8,128)S(1)} fusion(f32[4,1024,128]{1,2,0:T(8,128)S(1)} %get-tuple-element.159, s32[512]{0:T(512)S(1)} %bitcast.71, pred[]{:T(512)S(6)} %compare.12, bf16[512,128]{0,1:T(8,128)(2,1)S(1)} %fusion.95, bf16[4,512]{1,0:T(4,128)(2,1)S(1)} %dynamic-slice_bitcast_fusion.2), kind=kOutput, calls=%fused_computation.2.clone.1 | convolution fusion | flops 538705920 | bytes 4331521 | tf_op jit(solution)/shard_map/while/body/eval_jaxpr/pr,frz->fpz/dot_general | solution.py:85
  42.5 1.2 %bitcast_add_fusion.2 = f32[4,1024,128]{1,2,0:T(8,128)S(1)} fusion(f32[4,1024,128]{1,2,0:T(8,128)S(1)} %get-tuple-element.159, s32[512]{0:T(512)S(1)} %bitcast.71, pred[]{:T(512)S(6)} %compare.12, bf16[512,128]{0,1:T(8,128)(2,1)S(1)} %fusion.95, bf16[4,512]{1,0:T(4,128)(2,1)S(1)} %dynamic-slice_bitcast_fusion.2), kind=kOutput, calls=%fused_computation.2.clone.1 | convolution fusion | flops 538705920 | bytes 4331521 | tf_op jit(solution)/shard_map/while/body/eval_jaxpr/pr,frz->fpz/dot_general | solution.py:85
  43.9 1.2 %bitcast_add_fusion.2 = f32[4,1024,128]{1,2,0:T(8,128)S(1)} fusion(f32[4,1024,128]{1,2,0:T(8,128)S(1)} %get-tuple-element.159, s32[512]{0:T(512)S(1)} %bitcast.71, pred[]{:T(512)S(6)} %compare.12, bf16[512,128]{0,1:T(8,128)(2,1)S(1)} %fusion.95, bf16[4,512]{1,0:T(4,128)(2,1)S(1)} %dynamic-slice_bitcast_fusion.2), kind=kOutput, calls=%fused_computation.2.clone.1 | convolution fusion | flops 538705920 | bytes 4331521 | tf_op jit(solution)/shard_map/while/body/eval_jaxpr/pr,frz->fpz/dot_general | solution.py:85
  45.2 1.2 %bitcast_add_fusion.2 = f32[4,1024,128]{1,2,0:T(8,128)S(1)} fusion(f32[4,1024,128]{1,2,0:T(8,128)S(1)} %get-tuple-element.159, s32[512]{0:T(512)S(1)} %bitcast.71, pred[]{:T(512)S(6)} %compare.12, bf16[512,128]{0,1:T(8,128)(2,1)S(1)} %fusion.95, bf16[4,512]{1,0:T(4,128)(2,1)S(1)} %dynamic-slice_bitcast_fusion.2), kind=kOutput, calls=%fused_computation.2.clone.1 | convolution fusion | flops 538705920 | bytes 4331521 | tf_op jit(solution)/shard_map/while/body/eval_jaxpr/pr,frz->fpz/dot_general | solution.py:85
  46.5 1.8 %copy.28 = f32[4,1024,128]{2,1,0:T(8,128)} copy(f32[4,1024,128]{1,2,0:T(8,128)S(1)} %get-tuple-element.85) | data formatting | bytes 4194304 | tf_op jit(solution)/shard_map/while | solution.py:91
  48.3 3.5 %fusion.30 = f32[4,32,32,128]{3,2,1,0:T(8,128)S(1)} fusion(f32[4,32,32,128]{3,2,1,0:T(8,128)} %bitcast.69, f32[128]{0:T(128)S(1)} %select_reduce_fusion), kind=kOutput, calls=%fused_computation.39 | convolution fusion | flops 805453824 | bytes 4194816 | tf_op jit(solution)/shard_map/fayz,wz->fayw/dot_general | solution.py:94
  51.8 1.2 %fusion.86 = (f32[4,16,32,128]{3,2,1,0:T(8,128)S(1)}, f32[4,16,32,128]{3,2,1,0:T(8,128)}) fusion(f32[4,32,32,128]{3,2,1,0:T(8,128)S(1)} %fusion.30), kind=kLoop, calls=%fused_computation.112 | loop fusion | bytes 4194304 | tf_op jit(solution)/shard_map/slice | solution.py:24
  53.0 3.7 %collective-permute-start.1 = (f32[4,16,32,128]{3,2,1,0:T(8,128)}, f32[4,16,32,128]{3,2,1,0:T(8,128)}, u32[]{:S(2)}, u32[]{:S(2)}) collective-permute-start(f32[4,16,32,128]{3,2,1,0:T(8,128)} %get-tuple-element.120), channel_id=1, source_target_pairs={{64,0},{128,64},{192,128},{256,192},{320,256},{384,320},{448,384},... | collective-permute-start | bytes 3145736 | tf_op jit(solution)/shard_map/ppermute | solution.py:29
  56.7 2.2 %collective-permute-start = (f32[4,16,32,128]{3,2,1,0:T(8,128)S(1)}, f32[4,16,32,128]{3,2,1,0:T(8,128)}, u32[]{:S(2)}, u32[]{:S(2)}) collective-permute-start(f32[4,16,32,128]{3,2,1,0:T(8,128)S(1)} %get-tuple-element.119), channel_id=1, source_target_pairs={{0,64},{64,128},{128,192},{192,256},{256,320},{320,384},{384,448},... | collective-permute-start | bytes 3145736 | tf_op jit(solution)/shard_map/ppermute | solution.py:27
  59.1 21.3 %collective-permute-done.1 = f32[4,16,32,128]{3,2,1,0:T(8,128)} collective-permute-done((f32[4,16,32,128]{3,2,1,0:T(8,128)}, f32[4,16,32,128]{3,2,1,0:T(8,128)}, u32[]{:S(2)}, u32[]{:S(2)}) %collective-permute-start.1) | collective-permute-done | bytes 1048608 | tf_op jit(solution)/shard_map/ppermute | solution.py:29
  80.4 4.4 %collective-permute-done = f32[4,16,32,128]{3,2,1,0:T(8,128)} collective-permute-done((f32[4,16,32,128]{3,2,1,0:T(8,128)S(1)}, f32[4,16,32,128]{3,2,1,0:T(8,128)}, u32[]{:S(2)}, u32[]{:S(2)}) %collective-permute-start) | collective-permute-done | bytes 1048608 | tf_op jit(solution)/shard_map/ppermute | solution.py:27
  84.8 2.1 %pad_maximum_fusion = f32[4,64,32,128]{3,2,1,0:T(8,128)S(1)} fusion(f32[4,16,32,128]{3,2,1,0:T(8,128)} %collective-permute-done.1, f32[4,32,32,128]{3,2,1,0:T(8,128)S(1)} %fusion.30, f32[4,16,32,128]{3,2,1,0:T(8,128)} %collective-permute-done), kind=kLoop, calls=%fused_computation.22 | loop fusion | flops 2097152 | bytes 8388608 | tf_op jit(solution)/shard_map/concatenate | solution.py:25
  86.9 4.6 %fusion.19 = f32[4,32,32,128]{3,1,2,0:T(8,128)S(1)} fusion(f32[4,64,32,128]{3,2,1,0:T(8,128)S(1)} %pad_maximum_fusion, f32[32]{0:T(128)S(1)} %get-tuple-element.106, s32[32]{0:T(128)S(1)} %get-tuple-element.121, s32[64]{0:T(128)S(1)} %iota_add_fusion.2), kind=kOutput, calls=%fused_computation.29 | convolution fusion | flops 402671616 | bytes 6291968 | tf_op jit(solution)/shard_map/fayz,ba->fbyz/dot_general | solution.py:108
  91.5 1.2 %fusion.85 = (f32[4,32,16,128]{3,1,2,0:T(8,128)S(1)}, f32[4,32,16,128]{3,1,2,0:T(8,128)}) fusion(f32[4,32,32,128]{3,1,2,0:T(8,128)S(1)} %fusion.19), kind=kLoop, calls=%fused_computation.111 | loop fusion | bytes 4194304 | tf_op jit(solution)/shard_map/slice | solution.py:24
  92.7 1.9 %collective-permute-start.3 = (f32[4,32,16,128]{3,1,2,0:T(8,128)}, f32[4,32,16,128]{3,1,2,0:T(8,128)}, u32[]{:S(2)}, u32[]{:S(2)}) collective-permute-start(f32[4,32,16,128]{3,1,2,0:T(8,128)} %get-tuple-element.118), channel_id=1, source_target_pairs={{1,0},{2,1},{3,2},{4,3},{5,4},{6,5},{7,6},{8,7},{9,8},{10,9},{11,1... | collective-permute-start | bytes 3145736 | tf_op jit(solution)/shard_map/ppermute | solution.py:29
  94.6 2.6 %collective-permute-start.2 = (f32[4,32,16,128]{3,1,2,0:T(8,128)S(1)}, f32[4,32,16,128]{3,1,2,0:T(8,128)}, u32[]{:S(2)}, u32[]{:S(2)}) collective-permute-start(f32[4,32,16,128]{3,1,2,0:T(8,128)S(1)} %get-tuple-element.117), channel_id=1, source_target_pairs={{0,1},{1,2},{2,3},{3,4},{4,5},{5,6},{6,7},{7,8},{8,9},{9,10},{10,1... | collective-permute-start | bytes 3145736 | tf_op jit(solution)/shard_map/ppermute | solution.py:27
  97.2 10.0 %collective-permute-done.3 = f32[4,32,16,128]{3,1,2,0:T(8,128)} collective-permute-done((f32[4,32,16,128]{3,1,2,0:T(8,128)}, f32[4,32,16,128]{3,1,2,0:T(8,128)}, u32[]{:S(2)}, u32[]{:S(2)}) %collective-permute-start.3) | collective-permute-done | bytes 1048608 | tf_op jit(solution)/shard_map/ppermute | solution.py:29
  107.2 5.7 %collective-permute-done.2 = f32[4,32,16,128]{3,1,2,0:T(8,128)} collective-permute-done((f32[4,32,16,128]{3,1,2,0:T(8,128)S(1)}, f32[4,32,16,128]{3,1,2,0:T(8,128)}, u32[]{:S(2)}, u32[]{:S(2)}) %collective-permute-start.2) | collective-permute-done | bytes 1048608 | tf_op jit(solution)/shard_map/ppermute | solution.py:27
  112.9 2.1 %pad_maximum_fusion.1 = f32[4,32,64,128]{3,1,2,0:T(8,128)S(1)} fusion(f32[4,32,16,128]{3,1,2,0:T(8,128)} %collective-permute-done.3, f32[4,32,32,128]{3,1,2,0:T(8,128)S(1)} %fusion.19, f32[4,32,16,128]{3,1,2,0:T(8,128)} %collective-permute-done.2), kind=kLoop, calls=%fused_computation.23 | loop fusion | flops 2097152 | bytes 8388608 | tf_op jit(solution)/shard_map/concatenate | solution.py:25
  115.0 5.9 %multiply_bitcast_fusion = f32[4,32,32,128]{3,2,1,0:T(8,128)} fusion(f32[4,32,64,128]{3,1,2,0:T(8,128)S(1)} %pad_maximum_fusion.1, f32[32]{0:T(128)S(1)} %get-tuple-element.105, s32[32]{0:T(128)S(1)} %get-tuple-element.122, s32[64]{0:T(128)S(1)} %iota_add_fusion.5), kind=kOutput, calls=%fused_computation.28 | convolution fusion | flops 403195904 | bytes 6291968 | tf_op jit(solution)/shard_map/fayz,cy->facz/dot_general | solution.py:116
  (49 shorter events, 2.6 us)
Async XLA Ops:
  0.0 35.4 %copy-start = (bf16[4,16]{1,0:T(4,128)(2,1)S(1)}, bf16[4,16]{1,0:T(4,128)(2,1)}, u32[]{:S(2)}) copy-start(bf16[4,16]{1,0:T(4,128)(2,1)} %param.9) | copy-start | bytes 388
  0.0 19.3 %all-to-all-start.1 = ((s32[1,1,64,64]{3,1,0,2:T(1,128)}), s32[1,1,64,64]{3,1,0,2:T(1,128)S(1)}, u32[]{:S(2)}, u32[]{:S(2)}) async-start(s32[1,1,64,64]{3,1,0,2:T(1,128)} %bitcast.73), calls=%async_computation.1 | async-start | bytes 65536 | tf_op jit(solution)/shard_map/all_to_all | solution.py:62
  19.3 15.9 %all-to-all-start = ((bf16[64,2,512]{2,1,0:T(2,128)(2,1)}), bf16[64,2,512]{2,1,0:T(2,128)(2,1)S(1)}, u32[]{:S(2)}, u32[]{:S(2)}) async-start(bf16[64,2,512]{2,1,0:T(2,128)(2,1)} %reshape.130), calls=%async_computation | async-start | bytes 262144 | tf_op jit(solution)/shard_map/all_to_all | solution.py:61
  53.0 27.4 %collective-permute-start.1 = (f32[4,16,32,128]{3,2,1,0:T(8,128)}, f32[4,16,32,128]{3,2,1,0:T(8,128)}, u32[]{:S(2)}, u32[]{:S(2)}) collective-permute-start(f32[4,16,32,128]{3,2,1,0:T(8,128)} %get-tuple-element.120), channel_id=1, source_target_pairs={{64,0},{128,64},{192,128},{256,192},{320,256},{384,320},{448,384},... | collective-permute-start | bytes 3145736 | tf_op jit(solution)/shard_map/ppermute | solution.py:29
  56.7 28.1 %collective-permute-start = (f32[4,16,32,128]{3,2,1,0:T(8,128)S(1)}, f32[4,16,32,128]{3,2,1,0:T(8,128)}, u32[]{:S(2)}, u32[]{:S(2)}) collective-permute-start(f32[4,16,32,128]{3,2,1,0:T(8,128)S(1)} %get-tuple-element.119), channel_id=1, source_target_pairs={{0,64},{64,128},{128,192},{192,256},{256,320},{320,384},{384,448},... | collective-permute-start | bytes 3145736 | tf_op jit(solution)/shard_map/ppermute | solution.py:27
  92.7 14.5 %collective-permute-start.3 = (f32[4,32,16,128]{3,1,2,0:T(8,128)}, f32[4,32,16,128]{3,1,2,0:T(8,128)}, u32[]{:S(2)}, u32[]{:S(2)}) collective-permute-start(f32[4,32,16,128]{3,1,2,0:T(8,128)} %get-tuple-element.118), channel_id=1, source_target_pairs={{1,0},{2,1},{3,2},{4,3},{5,4},{6,5},{7,6},{8,7},{9,8},{10,9},{11,1... | collective-permute-start | bytes 3145736 | tf_op jit(solution)/shard_map/ppermute | solution.py:29
  94.6 18.3 %collective-permute-start.2 = (f32[4,32,16,128]{3,1,2,0:T(8,128)S(1)}, f32[4,32,16,128]{3,1,2,0:T(8,128)}, u32[]{:S(2)}, u32[]{:S(2)}) collective-permute-start(f32[4,32,16,128]{3,1,2,0:T(8,128)S(1)} %get-tuple-element.117), channel_id=1, source_target_pairs={{0,1},{1,2},{2,3},{3,4},{4,5},{5,6},{6,7},{7,8},{8,9},{9,10},{10,1... | collective-permute-start | bytes 3145736 | tf_op jit(solution)/shard_map/ppermute | solution.py:27
where the time goes:
time: 121 us
  waiting for transfers between devices  56.3 us (47%)
  starting transfers between devices  26.6 us (22%)
  matrix products  23.9 us (20%)
  other arithmetic  7.36 us (6%)
  local copies, waits for them, and re-layouts  6.12 us (5%)
    ppermute x2, waiting for transfers between devices, padded_2(): lax.ppermute(head, axis, [((i + 1) % count, i) for i in range(ends)])  31.3 us
    all_to_all x1, starting transfers between devices, on_device(): lax.all_to_all(cell_index, 'cr', split_axis=2, concat_axis=1, tiled=True)  10.7 us
    ppermute x2, waiting for transfers between devices, padded_2(): lax.ppermute(tail, axis, [(i, (i + 1) % count) for i in range(ends)])  10.1 us
    dot_general x8, matrix products, add_block(): jnp.einsum('pr,frz->fpz', pick_plane, weighted, preferred_element_type=jn...  9.77 us
    all_to_all x1, waiting for transfers between devices, on_device(): lax.all_to_all(kept[None, None], 'cr', split_axis=2, concat_axis=1, tiled...  8.94 us
    all_to_all x1, waiting for transfers between devices, on_device(): lax.all_to_all(cell_index, 'cr', split_axis=2, concat_axis=1, tiled=True)  5.95 us
    dot_general x1, matrix products, on_device(): jnp.einsum('fayz,cy->facz', padded, band_cross, precision=lax.Precision.H...  5.86 us
    ppermute x2, starting transfers between devices, padded_2(): lax.ppermute(head, axis, [((i + 1) % count, i) for i in range(ends)])  5.57 us
  transfers between devices with their start and end apart: 6, of which 6 were waited for; matrix products, arithmetic and copies ran while one was open for 3% of the time, Pallas kernels for 0%

commit v1 on v0

v1 whole, which is shorter than its diff:
```python
import math

import jax
import jax.numpy as jnp
import ml_dtypes
import numpy as np
from jax import lax
from jax.experimental import pallas as pl
from jax.experimental.pallas import tpu as pltpu
from jax.sharding import PartitionSpec as P

CA = 32
CY = 32
NZ = 128
COMP = 4
HALF = 16
NX = 384
NY = 2048
SLOTS = 4096
FZ = COMP * NZ
BF = jnp.bfloat16
F32 = jnp.float32
NT = (((1,), (1,)), ((), ()))

VOLUME = 256.0
SIGMA = 0.75 * HALF
TAPS = [math.exp(-k * k / (2.0 * SIGMA * SIGMA)) for k in range(HALF + 1)]
STRETCH = 1.8433
HELD = [float(np.float32(STRETCH * t).astype(ml_dtypes.bfloat16)) for t in TAPS]
_W = [1.0] + [2.0] * HALF
UNDO = sum(w * h * t for w, h, t in zip(_W, HELD, TAPS)) / sum(w * h * h for w, h in zip(_W, HELD))


def band(out_pos, in_pos):
    gap = np.abs(np.asarray(in_pos)[None, :] - np.asarray(out_pos)[:, None])
    held = np.asarray(HELD + [0.0], np.float32)
    return held[np.minimum(gap, HALF + 1)]


OWN, BELOW, ABOVE = np.arange(32), np.arange(-16, 0), np.arange(32, 48)
ROWS = 16


def _kx():
    pieces = []
    for p in (OWN, BELOW, ABOVE):
        b = band(OWN, p)
        n = b.shape[1]
        m = np.zeros((32, 8, 8, n), np.float32)
        for y in range(8):
            m[:, y, y, :] = b
        pieces.append(m.reshape(256, 8 * n))
    return np.concatenate(pieces, axis=1).astype(ml_dtypes.bfloat16)


def _ky():
    eye = np.eye(4, dtype=np.float32)
    return np.concatenate([np.kron(eye, band(OWN, p)) for p in (OWN, BELOW, ABOVE)], axis=1).astype(ml_dtypes.bfloat16)


def _kz():
    b = band(np.arange(NZ), np.arange(NZ)).T
    return np.concatenate([b, b], axis=0).astype(ml_dtypes.bfloat16)


def deposit_kernel(own_ref, below_ref, above_ref, kx_ref, e_ref, wt, acc):
    lists = (own_ref, below_ref, above_ref)
    one, zero = jnp.ones((), BF), jnp.zeros((), BF)

    def rows_iota(n, width):
        return lax.broadcasted_iota(jnp.int32, (n, width), 0).astype(F32).astype(BF)

    width = 1024
    for l, ref in enumerate(lists):
        for b in range(SLOTS // width):
            ks = pl.ds(b * width, width)
            hit = jnp.broadcast_to(ref[4:5, ks], (NZ, width)) == rows_iota(NZ, width)
            for f in range(COMP):
                s = jnp.broadcast_to(ref[f : f + 1, ks], (NZ, width))
                wt[l, f * NZ : (f + 1) * NZ, ks] = jnp.where(hit, s, zero)
    for c in range(CY // ROWS):
        for l, ref in enumerate(lists):
            n = 32 if l == 0 else 16
            x0 = (0, 16, 0)[l]
            r0 = (0, ROWS * 32, ROWS * 48)[l]
            y = ref[5:6, :].astype(F32) - float(c * ROWS)
            x = ref[6:7, :].astype(F32) - float(x0)
            ok = (x >= 0) & (x < n)
            parts = []
            for i in range(ROWS):
                key = jnp.where(ok & (y == i), x, -1.0).astype(BF)
                parts.append(jnp.where(jnp.broadcast_to(key, (n, SLOTS)) == rows_iota(n, SLOTS), one, zero))
            picks = jnp.concatenate(parts, axis=0)
            acc[r0 : r0 + ROWS * n, :] = lax.dot_general(picks, wt[l], NT, preferred_element_type=F32)
        done = []
        for i in range(ROWS // 8):
            d = jnp.concatenate(
                [
                    acc[i * 256 : (i + 1) * 256, :],
                    acc[ROWS * 32 + i * 128 : ROWS * 32 + (i + 1) * 128, :],
                    acc[ROWS * 48 + i * 128 : ROWS * 48 + (i + 1) * 128, :],
                ],
                axis=0,
            )
            high = d.astype(BF)
            low = (d - high.astype(F32)).astype(BF)
            r = jnp.dot(kx_ref[...], high, preferred_element_type=F32)
            r += jnp.dot(kx_ref[...], low, preferred_element_type=F32)
            done.append(r.reshape(CA, 8, FZ))
        e_ref[:, c * ROWS : (c + 1) * ROWS, :] = jnp.concatenate(done, axis=1).astype(BF)


def weight_sum(pos, extent):
    total = jnp.zeros(pos.shape, F32)
    for k in range(-HALF, HALF + 1):
        inside = (pos + k >= 0) & (pos + k < extent)
        total = total + jnp.where(inside, TAPS[abs(k)], 0.0)
    return total


def finish_kernel(at_ref, own_ref, below_ref, above_ref, ky_ref, kz_ref, out_ref):
    step = pl.program_id(0)
    layers = own_ref.shape[0]
    pos_z = lax.broadcasted_iota(jnp.int32, (8, NZ), 1)
    pos_y = lax.broadcasted_iota(jnp.int32, (CY, NZ), 0) + at_ref[1] * CY
    yz = (weight_sum(pos_y, NY) * weight_sum(pos_z, NZ)[0:1, :])
    for g in range(layers // 4):
        xs = slice(g * 4, g * 4 + 4)
        rhs = jnp.concatenate(
            [
                own_ref[xs].reshape(128, FZ),
                below_ref[xs].reshape(64, FZ),
                above_ref[xs].reshape(64, FZ),
            ],
            axis=0,
        )
        v = jnp.dot(ky_ref[...], rhs, preferred_element_type=F32)
        v = jnp.concatenate([v[:, f * NZ : (f + 1) * NZ] for f in range(COMP)], axis=0)
        high = v.astype(BF)
        low = (v - high.astype(F32)).astype(BF)
        r = jnp.dot(jnp.concatenate([high, low], axis=1), kz_ref[...], preferred_element_type=F32)
        pos_x = lax.broadcasted_iota(jnp.int32, (4, 8, NZ), 0) + (at_ref[0] * CA + step * layers + g * 4)
        scale = (VOLUME * UNDO**3) / (weight_sum(pos_x, NX)[:, 0:1, :] * yz[None])
        for f in range(COMP):
            out_ref[f, xs] = r[f * 128 : (f + 1) * 128].reshape(4, CY, NZ) * scale


VMEM_SPEC = pl.BlockSpec(memory_space=pltpu.VMEM)
LAYERS = 8


def on_device(parcels, cell_index, counts, coupling):
    bricks = lax.axis_size("cr")
    slabs = lax.axis_size("ax")
    capacity = parcels.shape[-1]
    slot_ids = jnp.arange(capacity, dtype=jnp.int32)
    live = slot_ids[None, :] < counts[0, 0][:, None]
    sources = jnp.einsum("fj,sjk->sfk", coupling, parcels[0, 0], preferred_element_type=F32)
    sources = jnp.where(live[:, None, :], sources.astype(BF), jnp.zeros((), BF))
    cell = cell_index[0, 0][:, None, :]
    places = jnp.concatenate([cell % NZ, (cell // NZ) % CY, cell // (NZ * CY), cell * 0], axis=1).astype(F32).astype(BF)
    letters = jnp.concatenate([sources, places], axis=1)
    arrived = lax.all_to_all(letters, "cr", split_axis=0, concat_axis=0, tiled=True)
    own = arrived.transpose(1, 0, 2).reshape(8, SLOTS)
    below = lax.ppermute(own, "ax", [(i, i + 1) for i in range(slabs - 1)])
    above = lax.ppermute(own, "ax", [(i + 1, i) for i in range(slabs - 1)])
    fields = pl.pallas_call(
        deposit_kernel,
        out_shape=jax.ShapeDtypeStruct((CA, CY, FZ), BF),
        in_specs=[VMEM_SPEC] * 4,
        out_specs=VMEM_SPEC,
        scratch_shapes=[pltpu.VMEM((3, FZ, SLOTS), BF), pltpu.VMEM((ROWS * 64, FZ), F32)],
        compiler_params=pltpu.CompilerParams(vmem_limit_bytes=60 << 20),
        name="deposit",
    )(own, below, above, jnp.asarray(_kx()))
    left = lax.ppermute(fields[:, 16:], "cr", [(i, i + 1) for i in range(bricks - 1)])
    right = lax.ppermute(fields[:, :16], "cr", [(i + 1, i) for i in range(bricks - 1)])
    at = jnp.stack([lax.axis_index("ax"), lax.axis_index("cr")]).astype(jnp.int32)
    return pl.pallas_call(
        finish_kernel,
        grid=(CA // LAYERS,),
        out_shape=jax.ShapeDtypeStruct((COMP, CA, CY, NZ), F32),
        in_specs=[
            pl.BlockSpec(memory_space=pltpu.SMEM),
            pl.BlockSpec((LAYERS, CY, FZ), lambda i: (i, 0, 0)),
            pl.BlockSpec((LAYERS, 16, FZ), lambda i: (i, 0, 0)),
            pl.BlockSpec((LAYERS, 16, FZ), lambda i: (i, 0, 0)),
            pl.BlockSpec((128, 256), lambda i: (0, 0)),
            pl.BlockSpec((256, NZ), lambda i: (0, 0)),
        ],
        out_specs=pl.BlockSpec((COMP, LAYERS, CY, NZ), lambda i: (0, i, 0, 0)),
        compiler_params=pltpu.CompilerParams(vmem_limit_bytes=40 << 20),
        name="finish",
    )(at, fields, left, right, jnp.asarray(_ky()), jnp.asarray(_kz()))


def solution(mesh):
    return jax.shard_map(
        on_device,
        mesh=mesh,
        in_specs=(
            P("ax", "cr", None, None, None),
            P("ax", "cr", None, None),
            P("ax", "cr", None),
            P(),
        ),
        out_specs=P(None, "ax", "cr", None),
        check_vma=False,
    )
```

time: 121 us -> 68.1 us (0.56)
  waiting for transfers between devices: 56.3 us -> 15.3 us
  matrix products: 23.9 us -> 0.84 us
  blocking collectives: 0 us -> 19.5 us
  starting transfers between devices: 26.6 us -> 10.2 us
  Pallas kernels: 0 us -> 16.2 us
  other arithmetic: 7.36 us -> 3.06 us
  local copies, waits for them, and re-layouts: 6.12 us -> 2.53 us
    ppermute x4, waiting for transfers between devices: 41.4 us -> 15.3 us  [the longest x1 5.93 us: on_device(): lax.ppermute(fields[:, 16:], 'cr', [(i, i + 1) for i in range(bricks - 1)])]
    dot_general x12 -> x1, matrix products: 23.9 us -> 0.84 us  [on_device(): jnp.einsum('fj,sjk->sfk', coupling, parcels[0, 0], preferred_element_type...]
    all_to_all x0 -> x1, blocking collectives: none -> 19.5 us  [on_device(): lax.all_to_all(letters, 'cr', split_axis=0, concat_axis=0, tiled=True)]
    all_to_all x2 -> x0, starting transfers between devices: 16.2 us -> none  [the longest x1 10.7 us: on_device(): lax.all_to_all(cell_index, 'cr', split_axis=2, concat_axis=1, tiled=True)]
    pallas_call x0 -> x2, Pallas kernels: none -> 16.2 us  [the longest x1 12 us: on_device(): pl.pallas_call(deposit_kernel, out_shape=jax.ShapeDtypeStruct((CA, CY, FZ...]
    all_to_all x2 -> x0, waiting for transfers between devices: 14.9 us -> none  [the longest x1 8.94 us: on_device(): lax.all_to_all(kept[None, None], 'cr', split_axis=2, concat_axis=1, tiled...]
    concatenate x2 -> x1, other arithmetic: 4.16 us -> 0.09 us  [on_device(): letters = jnp.concatenate([sources, places], axis=1)]
    while x1 -> x0, local copies, waits for them, and re-layouts: 1.81 us -> none  [on_device(): fields, _ = lax.scan(add_block, start_fields, (source_blocks, place_blocks))]
  transfers between devices with their start and end apart: 6 -> 4, of which waited for: 6 -> 4; matrix products, arithmetic and copies ran while one was open for 3% -> 0% of each run, Pallas kernels for 0% -> 0%
where the time goes in v1:
time: 68.1 us; the launch traced here: 67.7 us
  blocking collectives  19.5 us (29%)
  Pallas kernels  16.2 us (24%)
  waiting for transfers between devices  15.3 us (22%)
  starting transfers between devices  10.2 us (15%)
  other arithmetic  3.06 us (4%)
  local copies, waits for them, and re-layouts  2.53 us (4%)
  matrix products  0.84 us (1%)
    all_to_all x1, blocking collectives, on_device(): lax.all_to_all(letters, 'cr', split_axis=0, concat_axis=0, tiled=True)  19.5 us
    pallas_call x1, Pallas kernels, on_device(): pl.pallas_call(deposit_kernel, out_shape=jax.ShapeDtypeStruct((CA, CY, FZ...  12 us
    ppermute x1, waiting for transfers between devices, on_device(): lax.ppermute(fields[:, 16:], 'cr', [(i, i + 1) for i in range(bricks - 1)])  5.93 us
    ppermute x1, waiting for transfers between devices, on_device(): below = lax.ppermute(own, 'ax', [(i, i + 1) for i in range(slabs - 1)])  4.89 us
    ppermute x1, waiting for transfers between devices, on_device(): lax.ppermute(fields[:, :16], 'cr', [(i + 1, i) for i in range(bricks - 1)])  4.18 us
    pallas_call x1, Pallas kernels, on_device(): pl.pallas_call(finish_kernel, grid=(CA // LAYERS,), out_shape=jax.ShapeDt...  4.13 us
    ppermute x1, starting transfers between devices, on_device(): above = lax.ppermute(own, 'ax', [(i + 1, i) for i in range(slabs - 1)])  3.67 us
    ppermute x1, starting transfers between devices, on_device(): lax.ppermute(fields[:, 16:], 'cr', [(i, i + 1) for i in range(bricks - 1)])  2.41 us
  transfers between devices with their start and end apart: 4, of which 4 were waited for; matrix products, arithmetic and copies ran while one was open for 0% of the time, Pallas kernels for 0%

profile of v1, /device:TPU:520, one launch (start us, length us, event | category | flops | bytes accessed | tf_op | source)
XLA Modules:
  0.0 67.7 jit_solution(17305515221428190247)
XLA Ops:
  0.0 0.0 copy-start
  0.0 0.8 %iota_compare_fusion = pred[64,64]{1,0:T(8,128)(4,1)S(1)} fusion(s32[64]{0:T(128)} %bitcast.16), kind=kLoop, calls=%fused_computation.19 | loop fusion | flops 4096 | bytes 4352 | tf_op jit(solution)/shard_map/lt | solution.py:157
  0.8 0.9 %and_select_fusion.3 = (s32[64,1,64]{2,1,0:T(1,128)S(1)}, s32[64,1,64]{2,1,0:T(1,128)S(1)}) fusion(s32[64,1,64]{2,1,0:T(1,128)} %bitcast.14), kind=kLoop, calls=%fused_computation.12 | loop fusion | flops 45056 | bytes 49152 | tf_op jit(solution)/shard_map/jit(remainder)/select_n | solution.py:161
  1.6 1.1 %and_select_fusion.1 = (s32[64,1,64]{2,1,0:T(1,128)S(1)}, s32[64,1,64]{2,1,0:T(1,128)S(1)}) fusion(s32[64,1,64]{2,1,0:T(1,128)S(1)} %get-tuple-element.6, s32[64,1,64]{2,1,0:T(1,128)} %bitcast.15), kind=kLoop, calls=%fused_computation.10 | loop fusion | flops 135168 | bytes 65536 | tf_op jit(solution)/shard_map/jit(remainder)/select_n | solution.py:161
  2.7 0.0 copy-done
  2.8 0.8 %fusion.1 = bf16[64,4,64]{2,1,0:T(4,128)(2,1)S(1)} fusion(bf16[1,1,64,16,64]{4,3,2,1,0:T(8,128)(2,1)S(1)} %copy-done, pred[64,64]{1,0:T(8,128)(4,1)S(1)} %iota_compare_fusion, bf16[4,16]{1,0:T(4,128)(2,1)} %param.10), kind=kOutput, calls=%fused_computation.2 | convolution fusion | flops 557056 | bytes 168064 | tf_op jit(solution)/shard_map/fj,sjk->sfk/dot_general | solution.py:158
  3.6 0.2 fusion.3
  3.8 0.1 pad_maximum_fusion
  3.9 0.2 reshape.276
  4.1 19.5 %all_to_all.5 = bf16[64,2,256]{2,1,0:T(2,128)(2,1)S(1)} all-to-all(bf16[64,2,256]{2,1,0:T(2,128)(2,1)S(1)} %reshape.276), channel_id=1, replica_groups=mesh['ax'=12,'cr'=64] {'cr'}, dimensions={0} | all-to-all | bytes 131072 | tf_op jit(solution)/shard_map/all_to_all | solution.py:163
  23.6 0.0 copy-start.2
  23.6 0.1 reshape.277
  23.7 0.2 reshape.274.own_ref
  23.9 0.0 copy-start.4
  23.9 3.7 %collective-permute-start.1 = (bf16[8,4096]{1,0:T(8,128)(2,1)S(1)}, bf16[8,4096]{1,0:T(8,128)(2,1)S(1)}, u32[]{:S(2)}, u32[]{:S(2)}) collective-permute-start(bf16[8,4096]{1,0:T(8,128)(2,1)S(1)} %reshape.274.own_ref), channel_id=1, source_target_pairs={{64,0},{128,64},{192,128},{256,192},{320,256},{384,320},{448,384},... | collective-permute-start | bytes 196616 | tf_op jit(solution)/shard_map/ppermute | solution.py:166
  27.6 2.2 %collective-permute-start = (bf16[8,4096]{1,0:T(8,128)(2,1)S(1)}, bf16[8,4096]{1,0:T(8,128)(2,1)S(1)}, u32[]{:S(2)}, u32[]{:S(2)}) collective-permute-start(bf16[8,4096]{1,0:T(8,128)(2,1)S(1)} %reshape.274.own_ref), channel_id=1, source_target_pairs={{0,64},{64,128},{128,192},{192,256},{256,320},{320,384},{384,448},... | collective-permute-start | bytes 196616 | tf_op jit(solution)/shard_map/ppermute | solution.py:165
  29.8 0.3 collective-permute-done.1.above_ref
  30.1 4.9 %collective-permute-done.below_ref = bf16[8,4096]{1,0:T(8,128)(2,1)S(1)} collective-permute-done((bf16[8,4096]{1,0:T(8,128)(2,1)S(1)}, bf16[8,4096]{1,0:T(8,128)(2,1)S(1)}, u32[]{:S(2)}, u32[]{:S(2)}) %collective-permute-start) | collective-permute-done | bytes 65568 | tf_op jit(solution)/shard_map/ppermute | solution.py:165
  35.0 0.0 copy-done.4
  35.0 0.0 copy-done.5
  35.0 0.6 copy-done.6
  35.6 12.0 %deposit.1.own_ref = bf16[32,32,512]{2,1,0:T(8,128)(2,1)} custom-call(bf16[8,4096]{1,0:T(8,128)(2,1)} %copy-done.4, bf16[8,4096]{1,0:T(8,128)(2,1)} %copy-done.6, bf16[8,4096]{1,0:T(8,128)(2,1)} %copy-done.5, bf16[256,512]{1,0:T(8,128)(2,1)} %constant.67.clone.kx_ref), custom_call_target="tpu_custom_call" | custom-call | tf_op jit(solution)/shard_map/deposit/pallas_call | solution.py:167
  47.6 1.4 %fusion.6 = (bf16[32,16,512]{2,1,0:T(8,128)(2,1)S(1)}, bf16[32,16,512]{2,1,0:T(8,128)(2,1)S(1)}) fusion(bf16[32,32,512]{2,1,0:T(8,128)(2,1)} %deposit.1.own_ref), kind=kLoop, calls=%fused_computation.23 | loop fusion | bytes 2097152 | tf_op jit(solution)/shard_map/slice | solution.py:177
  49.0 1.9 %collective-permute-start.3 = (bf16[32,16,512]{2,1,0:T(8,128)(2,1)S(1)}, bf16[32,16,512]{2,1,0:T(8,128)(2,1)S(1)}, u32[]{:S(2)}, u32[]{:S(2)}) collective-permute-start(bf16[32,16,512]{2,1,0:T(8,128)(2,1)S(1)} %get-tuple-element.7), channel_id=1, source_target_pairs={{1,0},{2,1},{3,2},{4,3},{5,4},{6,5},{7,6},{8,7},{9,8},{10,9},{11,1... | collective-permute-start | bytes 1572872 | tf_op jit(solution)/shard_map/ppermute | solution.py:177
  50.9 2.4 %collective-permute-start.2 = (bf16[32,16,512]{2,1,0:T(8,128)(2,1)S(1)}, bf16[32,16,512]{2,1,0:T(8,128)(2,1)S(1)}, u32[]{:S(2)}, u32[]{:S(2)}) collective-permute-start(bf16[32,16,512]{2,1,0:T(8,128)(2,1)S(1)} %get-tuple-element.8), channel_id=1, source_target_pairs={{0,1},{1,2},{2,3},{3,4},{4,5},{5,6},{6,7},{7,8},{8,9},{9,10},{10,1... | collective-permute-start | bytes 1572872 | tf_op jit(solution)/shard_map/ppermute | solution.py:176
  53.4 0.1 pad_add_fusion.at_ref
  53.4 4.2 %collective-permute-done.3.above_ref = bf16[32,16,512]{2,1,0:T(8,128)(2,1)S(1)} collective-permute-done((bf16[32,16,512]{2,1,0:T(8,128)(2,1)S(1)}, bf16[32,16,512]{2,1,0:T(8,128)(2,1)S(1)}, u32[]{:S(2)}, u32[]{:S(2)}) %collective-permute-start.3) | collective-permute-done | bytes 524320 | tf_op jit(solution)/shard_map/ppermute | solution.py:177
  57.6 5.9 %collective-permute-done.2.below_ref = bf16[32,16,512]{2,1,0:T(8,128)(2,1)S(1)} collective-permute-done((bf16[32,16,512]{2,1,0:T(8,128)(2,1)S(1)}, bf16[32,16,512]{2,1,0:T(8,128)(2,1)S(1)}, u32[]{:S(2)}, u32[]{:S(2)}) %collective-permute-start.2) | collective-permute-done | bytes 524320 | tf_op jit(solution)/shard_map/ppermute | solution.py:176
  63.5 0.0 copy-done.2
  63.5 0.0 copy-done.3
  63.5 0.0 copy-done.1
  63.6 4.1 %finish.1 = f32[4,32,32,128]{3,2,1,0:T(8,128)} custom-call(s32[2]{0:T(128)S(1)} %pad_add_fusion.at_ref, bf16[32,32,512]{2,1,0:T(8,128)(2,1)S(1)} %copy-done.1, bf16[32,16,512]{2,1,0:T(8,128)(2,1)S(1)} %collective-permute-done.2.below_ref, bf16[32,16,512]{2,1,0:T(8,128)(2,1)S(1)} %collective-permute-done.3.above_ref, bf16[128,256]{1,0:T(8,128)(2,1)S(1)} %copy-done.3, ...), custom_call_target="tpu_custom_call" | custom-call | tf_op jit(solution)/shard_map/finish/pallas_call | solution.py:179
  (6 shorter events, 0.0 us)
Async XLA Ops:
  0.0 2.8 %copy-start = (bf16[1,1,64,16,64]{4,3,2,1,0:T(8,128)(2,1)S(1)}, bf16[1,1,64,16,64]{4,3,2,1,0:T(8,128)(2,1)}, u32[]{:S(2)}) copy-start(bf16[1,1,64,16,64]{4,3,2,1,0:T(8,128)(2,1)} %param.7) | copy-start | bytes 393220
  23.6 40.0 %copy-start.2 = (bf16[256,128]{1,0:T(8,128)(2,1)S(1)}, bf16[256,128]{1,0:T(8,128)(2,1)}, u32[]{:S(2)}) copy-start(bf16[256,128]{1,0:T(8,128)(2,1)} %constant.69.clone.kz_ref) | copy-start | bytes 196612
  23.6 40.0 %copy-start.3 = (bf16[128,256]{1,0:T(8,128)(2,1)S(1)}, bf16[128,256]{1,0:T(8,128)(2,1)}, u32[]{:S(2)}) copy-start(bf16[128,256]{1,0:T(8,128)(2,1)} %constant.68.clone.ky_ref) | copy-start | bytes 196612
  23.9 11.1 %copy-start.4 = (bf16[8,4096]{1,0:T(8,128)(2,1)}, bf16[8,4096]{1,0:T(8,128)(2,1)S(1)}, u32[]{:S(2)}) copy-start(bf16[8,4096]{1,0:T(8,128)(2,1)S(1)} %reshape.274.own_ref) | copy-start | bytes 196612
  23.9 6.2 %collective-permute-start.1 = (bf16[8,4096]{1,0:T(8,128)(2,1)S(1)}, bf16[8,4096]{1,0:T(8,128)(2,1)S(1)}, u32[]{:S(2)}, u32[]{:S(2)}) collective-permute-start(bf16[8,4096]{1,0:T(8,128)(2,1)S(1)} %reshape.274.own_ref), channel_id=1, source_target_pairs={{64,0},{128,64},{192,128},{256,192},{320,256},{384,320},{448,384},... | collective-permute-start | bytes 196616 | tf_op jit(solution)/shard_map/ppermute | solution.py:166
  27.6 7.4 %collective-permute-start = (bf16[8,4096]{1,0:T(8,128)(2,1)S(1)}, bf16[8,4096]{1,0:T(8,128)(2,1)S(1)}, u32[]{:S(2)}, u32[]{:S(2)}) collective-permute-start(bf16[8,4096]{1,0:T(8,128)(2,1)S(1)} %reshape.274.own_ref), channel_id=1, source_target_pairs={{0,64},{64,128},{128,192},{192,256},{256,320},{320,384},{384,448},... | collective-permute-start | bytes 196616 | tf_op jit(solution)/shard_map/ppermute | solution.py:165
  30.1 4.9 %copy-start.5 = (bf16[8,4096]{1,0:T(8,128)(2,1)}, bf16[8,4096]{1,0:T(8,128)(2,1)S(1)}, u32[]{:S(2)}) copy-start(bf16[8,4096]{1,0:T(8,128)(2,1)S(1)} %collective-permute-done.1.above_ref) | copy-start | bytes 196612
  35.0 0.6 copy-start.6
  47.6 15.9 %copy-start.1 = (bf16[32,32,512]{2,1,0:T(8,128)(2,1)S(1)}, bf16[32,32,512]{2,1,0:T(8,128)(2,1)}, u32[]{:S(2)}) copy-start(bf16[32,32,512]{2,1,0:T(8,128)(2,1)} %deposit.1.own_ref) | copy-start | bytes 3145732
  49.0 8.6 %collective-permute-start.3 = (bf16[32,16,512]{2,1,0:T(8,128)(2,1)S(1)}, bf16[32,16,512]{2,1,0:T(8,128)(2,1)S(1)}, u32[]{:S(2)}, u32[]{:S(2)}) collective-permute-start(bf16[32,16,512]{2,1,0:T(8,128)(2,1)S(1)} %get-tuple-element.7), channel_id=1, source_target_pairs={{1,0},{2,1},{3,2},{4,3},{5,4},{6,5},{7,6},{8,7},{9,8},{10,9},{11,1... | collective-permute-start | bytes 1572872 | tf_op jit(solution)/shard_map/ppermute | solution.py:177
  50.9 12.6 %collective-permute-start.2 = (bf16[32,16,512]{2,1,0:T(8,128)(2,1)S(1)}, bf16[32,16,512]{2,1,0:T(8,128)(2,1)S(1)}, u32[]{:S(2)}, u32[]{:S(2)}) collective-permute-start(bf16[32,16,512]{2,1,0:T(8,128)(2,1)S(1)} %get-tuple-element.8), channel_id=1, source_target_pairs={{0,1},{1,2},{2,3},{3,4},{4,5},{5,6},{6,7},{7,8},{8,9},{9,10},{10,1... | collective-permute-start | bytes 1572872 | tf_op jit(solution)/shard_map/ppermute | solution.py:176

commit v2 on v1

v2 whole, which is shorter than its diff:
```python
import math

import jax
import jax.numpy as jnp
import ml_dtypes
import numpy as np
from jax import lax
from jax.experimental import pallas as pl
from jax.experimental.pallas import tpu as pltpu
from jax.sharding import PartitionSpec as P

CA = 32
CY = 32
NZ = 128
COMP = 4
HALF = 16
NX = 384
NY = 2048
SLOTS = 4096
FZ = COMP * NZ
BF = jnp.bfloat16
F32 = jnp.float32
NT = (((1,), (1,)), ((), ()))

VOLUME = 256.0
SIGMA = 0.75 * HALF
TAPS = [math.exp(-k * k / (2.0 * SIGMA * SIGMA)) for k in range(HALF + 1)]
STRETCH = 1.8433
HELD = [float(np.float32(STRETCH * t).astype(ml_dtypes.bfloat16)) for t in TAPS]
_W = [1.0] + [2.0] * HALF
UNDO = sum(w * h * t for w, h, t in zip(_W, HELD, TAPS)) / sum(w * h * h for w, h in zip(_W, HELD))


def band(out_pos, in_pos):
    gap = np.abs(np.asarray(in_pos)[None, :] - np.asarray(out_pos)[:, None])
    held = np.asarray(HELD + [0.0], np.float32)
    return held[np.minimum(gap, HALF + 1)]


OWN, BELOW, ABOVE = np.arange(32), np.arange(-16, 0), np.arange(32, 48)
ROWS = 16


def _kx():
    pieces = []
    for p in (OWN, BELOW, ABOVE):
        b = band(OWN, p)
        n = b.shape[1]
        m = np.zeros((32, 8, 8, n), np.float32)
        for y in range(8):
            m[:, y, y, :] = b
        pieces.append(m.reshape(256, 8 * n))
    return np.concatenate(pieces, axis=1).astype(ml_dtypes.bfloat16)


def _ky():
    eye = np.eye(4, dtype=np.float32)
    parts = (OWN[:16], OWN[16:], BELOW, ABOVE)
    return np.concatenate([np.kron(eye, band(OWN, p)) for p in parts], axis=1).astype(ml_dtypes.bfloat16)


def _kz():
    b = band(np.arange(NZ), np.arange(NZ)).T
    return np.concatenate([b, b], axis=0).astype(ml_dtypes.bfloat16)


def iota(shape, axis):
    return lax.broadcasted_iota(jnp.int32, shape, axis)


def weight_sum(pos, extent):
    total = jnp.zeros(pos.shape, F32)
    for k in range(-HALF, HALF + 1):
        inside = (pos + k >= 0) & (pos + k < extent)
        total = total + jnp.where(inside, TAPS[abs(k)], 0.0)
    return total


def split(v):
    high = v.astype(BF)
    return high, (v - high.astype(F32)).astype(BF)


def whole_kernel(
    parcels_ref, cell_ref, counts_ref, coupling_ref, kx_ref, ky_ref, kz_ref, out_ref,
    msg1, buf1, msg2, lists, flat, wt, picks, acc_own, acc_side, e_own, e_side, kxs, kys, sx, syz,
    send1, recv1, send2, recv2, send_ax, recv_ax, send_cr, recv_cr,
):
    a, c_at = lax.axis_index("ax"), lax.axis_index("cr")
    n_ax, n_cr = lax.axis_size("ax"), lax.axis_size("cr")
    y_at, g_at = c_at // 8, c_at % 8
    up, down = lax.rem(a + 1, n_ax), lax.rem(a + n_ax - 1, n_ax)
    right, left = lax.rem(c_at + 1, n_cr), lax.rem(c_at + n_cr - 1, n_cr)
    in_row = [(a, y_at * 8 + lax.rem(g_at + j, 8)) for j in range(1, 8)]
    in_column = [(a, lax.rem(y_at + j, 8) * 8 + g_at) for j in range(1, 8)]

    def remote(src, dst, send, recv, to):
        return pltpu.make_async_remote_copy(
            src_ref=src, dst_ref=dst, send_sem=send, recv_sem=recv, device_id=to, device_id_type=pl.DeviceIdType.MESH
        )

    barrier = pltpu.get_barrier_semaphore()
    partners = in_row + in_column + [(up, c_at), (down, c_at), (a, right), (a, left)]
    for to in partners:
        pl.semaphore_signal(barrier, inc=1, device_id=to, device_id_type=pl.DeviceIdType.MESH)

    one, zero = jnp.ones((), BF), jnp.zeros((), BF)

    r, s = iota((128, 4), 0), iota((128, 4), 1)
    spread = jnp.dot(((r & 7) == s).astype(F32).astype(BF), coupling_ref[...], preferred_element_type=F32).astype(BF)
    r, s = iota((16, 256), 0), iota((16, 256), 1)
    spread = jnp.dot(spread, ((s & 15) == r).astype(F32).astype(BF), preferred_element_type=F32)
    r, s = iota((128, 256), 0), iota((128, 256), 1)
    mix = jnp.where((r >> 3) == (s >> 4), spread, 0.0).astype(BF)
    eye = (iota((64, 64), 0) == iota((64, 64), 1)).astype(F32).astype(BF)
    counts = jnp.broadcast_to(counts_ref[...].astype(F32), (64, 64)).astype(BF)
    counts = lax.dot_general(eye, counts, NT, preferred_element_type=F32)
    live = iota((64, 64), 1).astype(F32) < counts
    cell = cell_ref[...]
    codes = []
    for code in (jnp.where(live, cell & 127, -1), (cell >> 7) & 31, cell >> 12):
        code = code.astype(F32)
        codes.append(jnp.concatenate([code[:32], code[32:]], axis=1))
    codes = jnp.concatenate(codes, axis=0).astype(BF)
    for group in range(2):
        records = []
        for b in range(16):
            d = (b % 4) * 8 + 4 * group + b // 4
            records.append(jnp.concatenate([parcels_ref[d], parcels_ref[d + 32]], axis=1))
        letter = jnp.dot(mix, jnp.concatenate(records, axis=0), preferred_element_type=F32)
        r, s = iota((128, 96), 0), iota((128, 96), 1)
        b = r >> 3
        choose = ((r & 7) == 4 + (s >> 5)) & ((s & 31) == (b & 3) * 8 + 4 * group + (b >> 2))
        letter += jnp.dot(choose.astype(F32).astype(BF), codes, preferred_element_type=F32)
        msg1[group * 4 : group * 4 + 4] = letter.astype(BF).reshape(4, 32, 128)

    pl.semaphore_wait(barrier, len(partners))
    first = []
    for j in range(1, 8):
        first.append(remote(msg1.at[lax.rem(g_at + j, 8)], buf1.at[g_at], send1.at[j - 1], recv1.at[j - 1], in_row[j - 1]))
        first[-1].start()
    buf1[g_at] = msg1[g_at]

    col = iota((256, 512), 1)
    gone = ((a == 0) & (col >= 256) & (col < 384)) | ((a == n_ax - 1) & (col >= 384))
    kxs[...] = jnp.where(gone, 0.0, kx_ref[...].astype(F32)).astype(BF)
    col = iota((128, 256), 1)
    gone = ((c_at == 0) & (col >= 128) & (col < 192)) | ((c_at == n_cr - 1) & (col >= 192))
    kys[...] = jnp.where(gone, 0.0, ky_ref[...].astype(F32)).astype(BF)
    sx[...] = 1.0 / weight_sum(iota((CA, NZ), 0) + a * CA, NX)
    syz[...] = (VOLUME * UNDO**3) / (
        weight_sum(iota((CY, NZ), 0) + c_at * CY, NY) * weight_sum(iota((8, NZ), 1), NZ)[0:1, :]
    )

    for copy in first:
        copy.wait_recv()
    near = iota((32, 128), 1) < 64
    halves = []
    for m in range(4):
        p, q = buf1[2 * m].astype(F32), buf1[2 * m + 1].astype(F32)
        halves.append((jnp.where(near, p, pltpu.roll(q, 64, 1)), jnp.where(near, pltpu.roll(p, 64, 1), q)))
    for h in range(2):
        for i in range(4):
            msg2[4 * h + i] = jnp.concatenate([halves[m][h][i * 8 : i * 8 + 8] for m in range(4)], axis=0).astype(BF)
    second = []
    for j in range(1, 8):
        second.append(
            remote(
                msg2.at[lax.rem(y_at + j, 8)], lists.at[0, y_at], send2.at[j - 1], recv2.at[j - 1], in_column[j - 1]
            )
        )
        second[-1].start()
    lists[0, y_at] = msg2[y_at]
    for copy in second:
        copy.wait_recv()
    along = [
        remote(lists.at[0], lists.at[1], send_ax.at[0], recv_ax.at[0], (up, c_at)),
        remote(lists.at[0], lists.at[2], send_ax.at[1], recv_ax.at[1], (down, c_at)),
    ]
    for copy in along:
        copy.start()

    def rows_iota(n, width):
        return iota((n, width), 0).astype(F32).astype(BF)

    def unfold(l):
        rows = lists[l].astype(F32).reshape(256, 128)
        flat[l] = jnp.concatenate([rows[b * 8 : b * 8 + 8] for b in range(32)], axis=1)
        width = 1024
        for b in range(SLOTS // width):
            ks = pl.ds(b * width, width)
            hit = jnp.broadcast_to(flat[l, 4:5, ks].astype(BF), (NZ, width)) == rows_iota(NZ, width)
            for f in range(COMP):
                source = jnp.broadcast_to(flat[l, f : f + 1, ks].astype(BF), (NZ, width))
                wt[l, f * NZ : (f + 1) * NZ, ks] = jnp.where(hit, source, zero)

    def picked(l, c):
        n, x0 = (32, 0) if l == 0 else (16, 16 if l == 1 else 0)
        y = flat[l, 5:6, :] - float(c * ROWS)
        x = flat[l, 6:7, :] - float(x0)
        ok = (x >= 0) & (x < n)
        parts = []
        for i in range(ROWS):
            key = jnp.where(ok & (y == i), x, -1.0).astype(BF)
            parts.append(jnp.where(jnp.broadcast_to(key, (n, SLOTS)) == rows_iota(n, SLOTS), one, zero))
        return jnp.concatenate(parts, axis=0)

    unfold(0)
    for c in range(2):
        acc_own[c] = lax.dot_general(picked(0, c), wt[0], NT, preferred_element_type=F32)
    for l in (1, 2):
        along[l - 1].wait_recv()
        unfold(l)
    across = []
    for h in range(2):
        fs = slice(h * 256, h * 256 + 256)
        for c in range(2):
            for l in (1, 2):
                if h == 0:
                    picks[c, l - 1] = picked(l, c)
                acc_side[l - 1] = lax.dot_general(picks[c, l - 1], wt[l, fs, :], NT, preferred_element_type=F32)
            done = []
            for i in range(2):
                own = acc_own[c, i * 256 : i * 256 + 256, fs]
                sides = [acc_side[k, i * 128 : i * 128 + 128, :] for k in range(2)]
                high, low = split(jnp.concatenate([own] + sides, axis=0))
                v = jnp.dot(kxs[...], high, preferred_element_type=F32)
                v += jnp.dot(kxs[...], low, preferred_element_type=F32)
                done.append(v.reshape(CA, 8, 256))
            e_own[h, c] = jnp.concatenate(done, axis=1).astype(BF)
            k = h * 2 + c
            across.append(remote(e_own.at[h, c], e_side.at[h, 1 - c], send_cr.at[k], recv_cr.at[k], (a, (left, right)[c])))
            across[-1].start()
    for h in range(2):
        across[2 * h].wait_recv()
        across[2 * h + 1].wait_recv()

        def layers(g, _):
            xs = pl.ds(g * 4, 4)
            rhs = [e_own[h, c, xs].reshape(64, 256) for c in range(2)] + [e_side[h, c, xs].reshape(64, 256) for c in range(2)]
            v = jnp.dot(kys[...], jnp.concatenate(rhs, axis=0), preferred_element_type=F32)
            high, low = split(jnp.concatenate([v[:, :128], v[:, 128:]], axis=0))
            v = jnp.dot(jnp.concatenate([high, low], axis=1), kz_ref[...], preferred_element_type=F32)
            v = v.reshape(2, 4, CY, NZ)
            for i in range(4):
                scale = syz[...] * sx[pl.ds(g * 4 + i, 1), :]
                for f in range(2):
                    out_ref[2 * h + f, g * 4 + i] = v[f, i] * scale
            return 0

        lax.fori_loop(0, CA // 4, layers, 0)
    for copy in first + second + along + across:
        copy.wait_send()


VMEM_SPEC = pl.BlockSpec(memory_space=pltpu.VMEM)


def on_device(parcels, cell_index, counts, coupling):
    return pl.pallas_call(
        whole_kernel,
        out_shape=jax.ShapeDtypeStruct((COMP, CA, CY, NZ), F32),
        in_specs=[VMEM_SPEC] * 7,
        out_specs=VMEM_SPEC,
        scratch_shapes=[
            pltpu.VMEM((8, 32, 128), BF),
            pltpu.VMEM((8, 32, 128), BF),
            pltpu.VMEM((8, 32, 128), BF),
            pltpu.VMEM((3, 8, 32, 128), BF),
            pltpu.VMEM((3, 8, SLOTS), F32),
            pltpu.VMEM((3, FZ, SLOTS), BF),
            pltpu.VMEM((2, 2, 256, SLOTS), BF),
            pltpu.VMEM((2, 512, FZ), F32),
            pltpu.VMEM((2, 256, 256), F32),
            pltpu.VMEM((2, 2, CA, 16, 256), BF),
            pltpu.VMEM((2, 2, CA, 16, 256), BF),
            pltpu.VMEM((256, 512), BF),
            pltpu.VMEM((128, 256), BF),
            pltpu.VMEM((CA, NZ), F32),
            pltpu.VMEM((CY, NZ), F32),
            pltpu.SemaphoreType.DMA((7,)),
            pltpu.SemaphoreType.DMA((7,)),
            pltpu.SemaphoreType.DMA((7,)),
            pltpu.SemaphoreType.DMA((7,)),
            pltpu.SemaphoreType.DMA((2,)),
            pltpu.SemaphoreType.DMA((2,)),
            pltpu.SemaphoreType.DMA((4,)),
            pltpu.SemaphoreType.DMA((4,)),
        ],
        compiler_params=pltpu.CompilerParams(vmem_limit_bytes=56 << 20, collective_id=0, has_side_effects=True),
        name="deposit_and_smooth",
    )(parcels[0, 0], cell_index[0, 0], counts[0], coupling, jnp.asarray(_kx()), jnp.asarray(_ky()), jnp.asarray(_kz()))


def solution(mesh):
    return jax.shard_map(
        on_device,
        mesh=mesh,
        in_specs=(
            P("ax", "cr", None, None, None),
            P("ax", "cr", None, None),
            P("ax", "cr", None),
            P(),
        ),
        out_specs=P(None, "ax", "cr", None),
        check_vma=False,
    )
```

time: 68.1 us -> 51.9 us (0.76)
  the two profiles are of different devices: /device:TPU:520 before, /device:TPU:1 now
where the time goes in v2:
time: 51.9 us; the launch traced here: 51.7 us
  Pallas kernels  48.7 us (94%)
  local copies, waits for them, and re-layouts  3.08 us (6%)
    pallas_call x1, Pallas kernels, on_device(): pl.pallas_call(whole_kernel, out_shape=jax.ShapeDtypeStruct((COMP, CA, CY...  48.7 us
    unnamed x1, local copies, waits for them, and re-layouts  3.08 us

profile of v2, /device:TPU:1, one launch (start us, length us, event | category | flops | bytes accessed | tf_op | source)
XLA Modules:
  0.0 51.7 jit_solution(2128585448636229555)
XLA Ops:
  0.0 48.7 %deposit_and_smooth.1 = f32[4,32,32,128]{3,2,1,0:T(8,128)} custom-call(bf16[64,16,64]{2,1,0:T(8,128)(2,1)} %bitcast.3, s32[64,64]{1,0:T(8,128)} %bitcast.4, s32[1,64]{1,0:T(1,128)} %bitcast.5, bf16[4,16]{1,0:T(4,128)(2,1)} %coupling_ref.1, bf16[256,512]{1,0:T(8,128)(2,1)} %constant.6.clone.kx_ref, bf16[128,256]{1,0:T(8,128)(2,1)} %constant.7.clone.ky_ref, ...), custom_call_target="tpu_custom_call" | custom-call | tf_op jit(solution)/shard_map/deposit_and_smooth/pallas_call | solution.py:260
  48.7 3.1 %copy.9 = f32[4,32,32,128]{3,2,1,0:T(8,128)} copy(f32[4,32,32,128]{3,2,1,0:T(8,128)} %deposit_and_smooth.1) | data formatting | bytes 4194304

commit v3 on v2

--- a/solution.py
+++ b/solution.py
@@ -31,37 +31,7 @@
 UNDO = sum(w * h * t for w, h, t in zip(_W, HELD, TAPS)) / sum(w * h * h for w, h in zip(_W, HELD))
 
 
-def band(out_pos, in_pos):
-    gap = np.abs(np.asarray(in_pos)[None, :] - np.asarray(out_pos)[:, None])
-    held = np.asarray(HELD + [0.0], np.float32)
-    return held[np.minimum(gap, HALF + 1)]
-
-
-OWN, BELOW, ABOVE = np.arange(32), np.arange(-16, 0), np.arange(32, 48)
 ROWS = 16
-
-
-def _kx():
-    pieces = []
-    for p in (OWN, BELOW, ABOVE):
-        b = band(OWN, p)
-        n = b.shape[1]
-        m = np.zeros((32, 8, 8, n), np.float32)
-        for y in range(8):
-            m[:, y, y, :] = b
-        pieces.append(m.reshape(256, 8 * n))
-    return np.concatenate(pieces, axis=1).astype(ml_dtypes.bfloat16)
-
-
-def _ky():
-    eye = np.eye(4, dtype=np.float32)
-    parts = (OWN[:16], OWN[16:], BELOW, ABOVE)
-    return np.concatenate([np.kron(eye, band(OWN, p)) for p in parts], axis=1).astype(ml_dtypes.bfloat16)
-
-
-def _kz():
-    b = band(np.arange(NZ), np.arange(NZ)).T
-    return np.concatenate([b, b], axis=0).astype(ml_dtypes.bfloat16)
 
 
 def iota(shape, axis):
@@ -76,14 +46,43 @@
     return total
 
 
+def taps_at(gap, where):
+    value = jnp.zeros(gap.shape, F32)
+    for k in range(HALF + 1):
+        value = jnp.where(gap == k, HELD[k], value)
+    return jnp.where(where, value, 0.0).astype(BF)
+
+
+def axial_band(below, above):
+    r, s = iota((256, 512), 0), iota((256, 512), 1)
+    own, low = s < 256, s < 384
+    row = jnp.where(own, s >> 5, (s >> 4) & 7)
+    layer = jnp.where(own, s & 31, jnp.where(low, (s & 15) - 16, (s & 15) + 32))
+    there = own | (jnp.where(low, below, above) > 0)
+    return taps_at(jnp.abs((r >> 3) - layer), ((r & 7) == row) & there)
+
+
+def cross_band(below, above):
+    r, s = iota((128, 256), 0), iota((128, 256), 1)
+    part = s >> 6
+    row = (s & 15) + jnp.where(part < 2, part * 16, jnp.where(part == 2, -16, 32))
+    there = (part < 2) | (jnp.where(part == 2, below, above) > 0)
+    return taps_at(jnp.abs((r & 31) - row), ((r >> 5) == ((s >> 4) & 3)) & there)
+
+
+def depth_band():
+    r, s = iota((256, NZ), 0), iota((256, NZ), 1)
+    return taps_at(jnp.abs((r & 127) - s), s >= 0)
+
+
 def split(v):
     high = v.astype(BF)
     return high, (v - high.astype(F32)).astype(BF)
 
 
 def whole_kernel(
-    parcels_ref, cell_ref, counts_ref, coupling_ref, kx_ref, ky_ref, kz_ref, out_ref,
-    msg1, buf1, msg2, lists, flat, wt, picks, acc_own, acc_side, e_own, e_side, kxs, kys, sx, syz,
+    parcels_hbm, cell_hbm, counts_hbm, coupling_hbm, out_ref,
+    parcels_ref, cell_ref, counts_ref, coupling_ref, msg1, buf1, msg2, lists, flat, wt, picks, acc_own, acc_side, e_own, e_side, kxs, kys, kzs, sx, syz, load,
     send1, recv1, send2, recv2, send_ax, recv_ax, send_cr, recv_cr,
 ):
     a, c_at = lax.axis_index("ax"), lax.axis_index("cr")
@@ -99,12 +98,22 @@
             src_ref=src, dst_ref=dst, send_sem=send, recv_sem=recv, device_id=to, device_id_type=pl.DeviceIdType.MESH
         )
 
+    loads = [
+        pltpu.make_async_copy(src, dst, load.at[k])
+        for k, (src, dst) in enumerate(
+            [(parcels_hbm, parcels_ref), (cell_hbm, cell_ref), (counts_hbm, counts_ref), (coupling_hbm, coupling_ref)]
+        )
+    ]
+    for copy in loads:
+        copy.start()
     barrier = pltpu.get_barrier_semaphore()
     partners = in_row + in_column + [(up, c_at), (down, c_at), (a, right), (a, left)]
     for to in partners:
         pl.semaphore_signal(barrier, inc=1, device_id=to, device_id_type=pl.DeviceIdType.MESH)
 
     one, zero = jnp.ones((), BF), jnp.zeros((), BF)
+    for copy in loads:
+        copy.wait()
 
     r, s = iota((128, 4), 0), iota((128, 4), 1)
     spread = jnp.dot(((r & 7) == s).astype(F32).astype(BF), coupling_ref[...], preferred_element_type=F32).astype(BF)
@@ -141,12 +150,9 @@
         first[-1].start()
     buf1[g_at] = msg1[g_at]
 
-    col = iota((256, 512), 1)
-    gone = ((a == 0) & (col >= 256) & (col < 384)) | ((a == n_ax - 1) & (col >= 384))
-    kxs[...] = jnp.where(gone, 0.0, kx_ref[...].astype(F32)).astype(BF)
-    col = iota((128, 256), 1)
-    gone = ((c_at == 0) & (col >= 128) & (col < 192)) | ((c_at == n_cr - 1) & (col >= 192))
-    kys[...] = jnp.where(gone, 0.0, ky_ref[...].astype(F32)).astype(BF)
+    kxs[...] = axial_band(a, n_ax - 1 - a)
+    kys[...] = cross_band(c_at, n_cr - 1 - c_at)
+    kzs[...] = depth_band()
     sx[...] = 1.0 / weight_sum(iota((CA, NZ), 0) + a * CA, NX)
     syz[...] = (VOLUME * UNDO**3) / (
         weight_sum(iota((CY, NZ), 0) + c_at * CY, NY) * weight_sum(iota((8, NZ), 1), NZ)[0:1, :]
@@ -235,20 +241,17 @@
         across[2 * h].wait_recv()
         across[2 * h + 1].wait_recv()
 
-        def layers(g, _):
-            xs = pl.ds(g * 4, 4)
+        for g in range(CA // 4):
+            xs = slice(g * 4, g * 4 + 4)
             rhs = [e_own[h, c, xs].reshape(64, 256) for c in range(2)] + [e_side[h, c, xs].reshape(64, 256) for c in range(2)]
             v = jnp.dot(kys[...], jnp.concatenate(rhs, axis=0), preferred_element_type=F32)
             high, low = split(jnp.concatenate([v[:, :128], v[:, 128:]], axis=0))
-            v = jnp.dot(jnp.concatenate([high, low], axis=1), kz_ref[...], preferred_element_type=F32)
+            v = jnp.dot(jnp.concatenate([high, low], axis=1), kzs[...], preferred_element_type=F32)
             v = v.reshape(2, 4, CY, NZ)
             for i in range(4):
-                scale = syz[...] * sx[pl.ds(g * 4 + i, 1), :]
+                scale = syz[...] * sx[g * 4 + i : g * 4 + i + 1, :]
                 for f in range(2):
                     out_ref[2 * h + f, g * 4 + i] = v[f, i] * scale
-            return 0
-
-        lax.fori_loop(0, CA // 4, layers, 0)
     for copy in first + second + along + across:
         copy.wait_send()
 
@@ -260,9 +263,13 @@
     return pl.pallas_call(
         whole_kernel,
         out_shape=jax.ShapeDtypeStruct((COMP, CA, CY, NZ), F32),
-        in_specs=[VMEM_SPEC] * 7,
+        in_specs=[pl.BlockSpec(memory_space=pltpu.HBM)] * 4,
         out_specs=VMEM_SPEC,
         scratch_shapes=[
+            pltpu.VMEM((64, 16, 64), BF),
+            pltpu.VMEM((64, 64), jnp.int32),
+            pltpu.VMEM((1, 64), jnp.int32),
+            pltpu.VMEM((COMP, 16), BF),
             pltpu.VMEM((8, 32, 128), BF),
             pltpu.VMEM((8, 32, 128), BF),
             pltpu.VMEM((8, 32, 128), BF),
@@ -276,8 +283,10 @@
             pltpu.VMEM((2, 2, CA, 16, 256), BF),
             pltpu.VMEM((256, 512), BF),
             pltpu.VMEM((128, 256), BF),
+            pltpu.VMEM((256, NZ), BF),
             pltpu.VMEM((CA, NZ), F32),
             pltpu.VMEM((CY, NZ), F32),
+            pltpu.SemaphoreType.DMA((4,)),
             pltpu.SemaphoreType.DMA((7,)),
             pltpu.SemaphoreType.DMA((7,)),
             pltpu.SemaphoreType.DMA((7,)),
@@ -287,9 +296,9 @@
             pltpu.SemaphoreType.DMA((4,)),
             pltpu.SemaphoreType.DMA((4,)),
         ],
-        compiler_params=pltpu.CompilerParams(vmem_limit_bytes=56 << 20, collective_id=0, has_side_effects=True),
+        compiler_params=pltpu.CompilerParams(vmem_limit_bytes=40 << 20, collective_id=0, has_side_effects=True),
         name="deposit_and_smooth",
-    )(parcels[0, 0], cell_index[0, 0], counts[0], coupling, jnp.asarray(_kx()), jnp.asarray(_ky()), jnp.asarray(_kz()))
+    )(parcels[0, 0], cell_index[0, 0], counts[0], coupling)
 
 
 def solution(mesh):

time: 51.9 us -> 49.4 us (0.952)
  Pallas kernels: 48.7 us -> 44.7 us
  local copies, waits for them, and re-layouts: 3.08 us -> 4.36 us
    pallas_call x1, Pallas kernels: 48.7 us -> 44.7 us  [on_device(): pl.pallas_call(whole_kernel, out_shape=jax.ShapeDtypeStruct((COMP, CA, CY...]
    unnamed x1 -> x9, local copies, waits for them, and re-layouts: 3.08 us -> 4.36 us
where the time goes in v3:
time: 49.4 us; the launch traced here: 49.1 us
  Pallas kernels  44.7 us (90%)
  local copies, waits for them, and re-layouts  4.36 us (9%)
    pallas_call x1, Pallas kernels, on_device(): pl.pallas_call(whole_kernel, out_shape=jax.ShapeDtypeStruct((COMP, CA, CY...  44.7 us
    unnamed x9, local copies, waits for them, and re-layouts  4.36 us

profile of v3, /device:TPU:1, one launch (start us, length us, event | category | flops | bytes accessed | tf_op | source)
XLA Modules:
  0.0 49.1 jit_solution(5661717253580630615)
XLA Ops:
  0.0 0.0 copy-start
  0.0 0.9 %copy-done = bf16[1,1,64,16,64]{4,3,2,1,0:T(8,128)(2,1)S(1)} copy-done((bf16[1,1,64,16,64]{4,3,2,1,0:T(8,128)(2,1)S(1)}, bf16[1,1,64,16,64]{4,3,2,1,0:T(8,128)(2,1)}, u32[]{:S(2)}) %copy-start) | copy-done | bytes 131096
  1.0 0.0 copy-start.1
  1.0 0.8 %copy-done.1 = s32[1,1,64,64]{3,2,1,0:T(8,128)S(1)} copy-done((s32[1,1,64,64]{3,2,1,0:T(8,128)S(1)}, s32[1,1,64,64]{3,2,1,0:T(8,128)}, u32[]{:S(2)}) %copy-start.1) | copy-done | bytes 16408
  1.7 0.0 copy-start.2
  1.7 0.7 %copy-done.2 = bf16[4,16]{1,0:T(4,128)(2,1)S(1)} copy-done((bf16[4,16]{1,0:T(4,128)(2,1)S(1)}, bf16[4,16]{1,0:T(4,128)(2,1)}, u32[]{:S(2)}) %copy-start.2) | copy-done | bytes 152
  2.4 0.0 copy-start.3
  2.4 0.7 %copy-done.3 = s32[1,1,64]{2,1,0:T(1,128)S(1)} copy-done((s32[1,1,64]{2,1,0:T(1,128)S(1)}, s32[1,1,64]{2,1,0:T(1,128)}, u32[]{:S(2)}) %copy-start.3) | copy-done | bytes 280
  3.0 44.7 %deposit_and_smooth.1 = f32[4,32,32,128]{3,2,1,0:T(8,128)S(1)} custom-call(bf16[64,16,64]{2,1,0:T(8,128)(2,1)S(1)} %bitcast.3, s32[64,64]{1,0:T(8,128)S(1)} %bitcast.4, s32[1,64]{1,0:T(1,128)S(1)} %bitcast.5, bf16[4,16]{1,0:T(4,128)(2,1)S(1)} %copy-done.2), custom_call_target="tpu_custom_call" | custom-call | tf_op jit(solution)/shard_map/deposit_and_smooth/pallas_call | solution.py:263
  47.8 1.3 %copy.6 = f32[4,32,32,128]{3,2,1,0:T(8,128)} copy(f32[4,32,32,128]{3,2,1,0:T(8,128)S(1)} %deposit_and_smooth.1) | data formatting | bytes 4194304
Async XLA Ops:
  0.0 0.9 %copy-start = (bf16[1,1,64,16,64]{4,3,2,1,0:T(8,128)(2,1)S(1)}, bf16[1,1,64,16,64]{4,3,2,1,0:T(8,128)(2,1)}, u32[]{:S(2)}) copy-start(bf16[1,1,64,16,64]{4,3,2,1,0:T(8,128)(2,1)} %param.4) | copy-start | bytes 393220
  1.0 0.8 %copy-start.1 = (s32[1,1,64,64]{3,2,1,0:T(8,128)S(1)}, s32[1,1,64,64]{3,2,1,0:T(8,128)}, u32[]{:S(2)}) copy-start(s32[1,1,64,64]{3,2,1,0:T(8,128)} %param.5) | copy-start | bytes 49156
  1.7 0.7 %copy-start.2 = (bf16[4,16]{1,0:T(4,128)(2,1)S(1)}, bf16[4,16]{1,0:T(4,128)(2,1)}, u32[]{:S(2)}) copy-start(bf16[4,16]{1,0:T(4,128)(2,1)} %coupling_hbm.1) | copy-start | bytes 388
  2.4 0.7 %copy-start.3 = (s32[1,1,64]{2,1,0:T(1,128)S(1)}, s32[1,1,64]{2,1,0:T(1,128)}, u32[]{:S(2)}) copy-start(s32[1,1,64]{2,1,0:T(1,128)} %param.6) | copy-start | bytes 772

commit v4 on v3

--- a/solution.py
+++ b/solution.py
@@ -64,10 +64,10 @@
 
 def cross_band(below, above):
     r, s = iota((128, 256), 0), iota((128, 256), 1)
-    part = s >> 6
-    row = (s & 15) + jnp.where(part < 2, part * 16, jnp.where(part == 2, -16, 32))
-    there = (part < 2) | (jnp.where(part == 2, below, above) > 0)
-    return taps_at(jnp.abs((r & 31) - row), ((r >> 5) == ((s >> 4) & 3)) & there)
+    part = s >> 5
+    row = (s & 7) + part * 8 - jnp.where(part < 4, 0, jnp.where(part < 6, 48, 16))
+    there = (part < 4) | (jnp.where(part < 6, below, above) > 0)
+    return taps_at(jnp.abs((r & 31) - row), ((r >> 5) == ((s >> 3) & 3)) & there)
 
 
 def depth_band():
@@ -82,7 +82,7 @@
 
 def whole_kernel(
     parcels_hbm, cell_hbm, counts_hbm, coupling_hbm, out_ref,
-    parcels_ref, cell_ref, counts_ref, coupling_ref, msg1, buf1, msg2, lists, flat, wt, picks, acc_own, acc_side, e_own, e_side, kxs, kys, kzs, sx, syz, load,
+    parcels_ref, cell_ref, counts_ref, coupling_ref, msg1, buf1, msg2, lists, flat, keys, wt, picks, acc_own, acc_side, e_own, e_side, kxs, kys, kzs, sx, syz, load,
     send1, recv1, send2, recv2, send_ax, recv_ax, send_cr, recv_cr,
 ):
     a, c_at = lax.axis_index("ax"), lax.axis_index("cr")
@@ -168,82 +168,97 @@
     for h in range(2):
         for i in range(4):
             msg2[4 * h + i] = jnp.concatenate([halves[m][h][i * 8 : i * 8 + 8] for m in range(4)], axis=0).astype(BF)
-    second = []
-    for j in range(1, 8):
-        second.append(
-            remote(
-                msg2.at[lax.rem(y_at + j, 8)], lists.at[0, y_at], send2.at[j - 1], recv2.at[j - 1], in_column[j - 1]
-            )
+    second = {}
+    for j in (4, 3, 5, 2, 6, 1, 7):
+        second[j] = remote(
+            msg2.at[lax.rem(y_at + j, 8)], lists.at[0, y_at], send2.at[j - 1], recv2.at[j - 1], in_column[j - 1]
         )
-        second[-1].start()
+        second[j].start()
     lists[0, y_at] = msg2[y_at]
-    for copy in second:
-        copy.wait_recv()
-    along = [
-        remote(lists.at[0], lists.at[1], send_ax.at[0], recv_ax.at[0], (up, c_at)),
-        remote(lists.at[0], lists.at[2], send_ax.at[1], recv_ax.at[1], (down, c_at)),
-    ]
-    for copy in along:
-        copy.start()
 
     def rows_iota(n, width):
         return iota((n, width), 0).astype(F32).astype(BF)
 
-    def unfold(l):
-        rows = lists[l].astype(F32).reshape(256, 128)
-        flat[l] = jnp.concatenate([rows[b * 8 : b * 8 + 8] for b in range(32)], axis=1)
-        width = 1024
-        for b in range(SLOTS // width):
-            ks = pl.ds(b * width, width)
-            hit = jnp.broadcast_to(flat[l, 4:5, ks].astype(BF), (NZ, width)) == rows_iota(NZ, width)
-            for f in range(COMP):
-                source = jnp.broadcast_to(flat[l, f : f + 1, ks].astype(BF), (NZ, width))
-                wt[l, f * NZ : (f + 1) * NZ, ks] = jnp.where(hit, source, zero)
-
-    def picked(l, c):
+    def source(j):
+        return lax.rem(y_at + 8 - j, 8)
+
+    def unfold(l, j, ks):
+        rows = lists[l, source(j)].astype(F32)
+        flat[l, :, ks] = jnp.concatenate([rows[b * 8 : b * 8 + 8] for b in range(4)], axis=1)
+        hit = jnp.broadcast_to(flat[l, 4:5, ks].astype(BF), (NZ, 512)) == rows_iota(NZ, 512)
+        for f in range(COMP):
+            term = jnp.broadcast_to(flat[l, f : f + 1, ks].astype(BF), (NZ, 512))
+            wt[l, f * NZ : (f + 1) * NZ, ks] = jnp.where(hit, term, zero)
         n, x0 = (32, 0) if l == 0 else (16, 16 if l == 1 else 0)
-        y = flat[l, 5:6, :] - float(c * ROWS)
-        x = flat[l, 6:7, :] - float(x0)
-        ok = (x >= 0) & (x < n)
+        y = jnp.broadcast_to(flat[l, 5:6, ks], (CY, 512))
+        x = jnp.broadcast_to(flat[l, 6:7, ks], (CY, 512)) - float(x0)
+        here = (y == iota((CY, 512), 0).astype(F32)) & (x >= 0) & (x < n)
+        keys[l, :, ks] = jnp.where(here, x, -1.0)
+
+    def picked(l, rows, ks, width):
+        n = 32 if l == 0 else 16
         parts = []
-        for i in range(ROWS):
-            key = jnp.where(ok & (y == i), x, -1.0).astype(BF)
-            parts.append(jnp.where(jnp.broadcast_to(key, (n, SLOTS)) == rows_iota(n, SLOTS), one, zero))
+        for i in rows:
+            key = jnp.broadcast_to(keys[l, i : i + 1, ks].astype(BF), (n, width))
+            parts.append(jnp.where(key == rows_iota(n, width), one, zero))
         return jnp.concatenate(parts, axis=0)
 
-    unfold(0)
-    for c in range(2):
-        acc_own[c] = lax.dot_general(picked(0, c), wt[0], NT, preferred_element_type=F32)
-    for l in (1, 2):
-        along[l - 1].wait_recv()
-        unfold(l)
+    along = {}
+    at = 0
+    order = ((0,), (1, 7), (2, 6), (3, 5), (4,))
+    for step in order:
+        for j in step:
+            if j:
+                second[j].wait_recv()
+            for k, to in ((0, up), (1, down)):
+                along[k, j] = remote(
+                    lists.at[0, source(j)], lists.at[1 + k, source(j)], send_ax.at[k, j], recv_ax.at[k, j], (to, c_at)
+                )
+                along[k, j].start()
+        for b, j in enumerate(step):
+            unfold(0, j, slice(at + b * 512, at + b * 512 + 512))
+        width = 512 * len(step)
+        ks = slice(at, at + width)
+        for c in range(2):
+            d = lax.dot_general(
+                picked(0, range(c * ROWS, c * ROWS + ROWS), ks, width), wt[0, :, ks], NT, preferred_element_type=F32
+            )
+            acc_own[c] = d if at == 0 else acc_own[c] + d
+        at += width
+    at = 0
+    for step in order:
+        for j in step:
+            for l in (1, 2):
+                along[l - 1, j].wait_recv()
+                unfold(l, j, slice(at, at + 512))
+            at += 512
     across = []
     for h in range(2):
         fs = slice(h * 256, h * 256 + 256)
-        for c in range(2):
+        for i in range(2):
             for l in (1, 2):
                 if h == 0:
-                    picks[c, l - 1] = picked(l, c)
-                acc_side[l - 1] = lax.dot_general(picks[c, l - 1], wt[l, fs, :], NT, preferred_element_type=F32)
-            done = []
-            for i in range(2):
+                    rows = [c * ROWS + i * 8 + k for c in range(2) for k in range(8)]
+                    picks[i, l - 1] = picked(l, rows, slice(0, SLOTS), SLOTS)
+                acc_side[l - 1] = lax.dot_general(picks[i, l - 1], wt[l, fs, :], NT, preferred_element_type=F32)
+            for c in range(2):
                 own = acc_own[c, i * 256 : i * 256 + 256, fs]
-                sides = [acc_side[k, i * 128 : i * 128 + 128, :] for k in range(2)]
+                sides = [acc_side[k, c * 128 : c * 128 + 128, :] for k in range(2)]
                 high, low = split(jnp.concatenate([own] + sides, axis=0))
                 v = jnp.dot(kxs[...], high, preferred_element_type=F32)
                 v += jnp.dot(kxs[...], low, preferred_element_type=F32)
-                done.append(v.reshape(CA, 8, 256))
-            e_own[h, c] = jnp.concatenate(done, axis=1).astype(BF)
-            k = h * 2 + c
-            across.append(remote(e_own.at[h, c], e_side.at[h, 1 - c], send_cr.at[k], recv_cr.at[k], (a, (left, right)[c])))
-            across[-1].start()
+                e_own[h, i, c] = v.astype(BF).reshape(16, 16, 256)
+                k = h * 4 + i * 2 + c
+                across.append(
+                    remote(e_own.at[h, i, c], e_side.at[h, i, 1 - c], send_cr.at[k], recv_cr.at[k], (a, (left, right)[c]))
+                )
+                across[-1].start()
     for h in range(2):
-        across[2 * h].wait_recv()
-        across[2 * h + 1].wait_recv()
-
+        for copy in across[4 * h : 4 * h + 4]:
+            copy.wait_recv()
         for g in range(CA // 4):
-            xs = slice(g * 4, g * 4 + 4)
-            rhs = [e_own[h, c, xs].reshape(64, 256) for c in range(2)] + [e_side[h, c, xs].reshape(64, 256) for c in range(2)]
+            xs = slice(g * 2, g * 2 + 2)
+            rhs = [e[h, i, c, xs].reshape(32, 256) for e in (e_own, e_side) for c in range(2) for i in range(2)]
             v = jnp.dot(kys[...], jnp.concatenate(rhs, axis=0), preferred_element_type=F32)
             high, low = split(jnp.concatenate([v[:, :128], v[:, 128:]], axis=0))
             v = jnp.dot(jnp.concatenate([high, low], axis=1), kzs[...], preferred_element_type=F32)
@@ -252,7 +267,7 @@
                 scale = syz[...] * sx[g * 4 + i : g * 4 + i + 1, :]
                 for f in range(2):
                     out_ref[2 * h + f, g * 4 + i] = v[f, i] * scale
-    for copy in first + second + along + across:
+    for copy in first + list(second.values()) + list(along.values()) + across:
         copy.wait_send()
 
 
@@ -260,6 +275,7 @@
 
 
 def on_device(parcels, cell_index, counts, coupling):
+    inputs = [pltpu.with_memory_space_constraint(v, pltpu.HBM) for v in (parcels[0, 0], cell_index[0, 0], counts[0], coupling)]
     return pl.pallas_call(
         whole_kernel,
         out_shape=jax.ShapeDtypeStruct((COMP, CA, CY, NZ), F32),
@@ -275,12 +291,13 @@
             pltpu.VMEM((8, 32, 128), BF),
             pltpu.VMEM((3, 8, 32, 128), BF),
             pltpu.VMEM((3, 8, SLOTS), F32),
+            pltpu.VMEM((3, CY, SLOTS), F32),
             pltpu.VMEM((3, FZ, SLOTS), BF),
             pltpu.VMEM((2, 2, 256, SLOTS), BF),
             pltpu.VMEM((2, 512, FZ), F32),
             pltpu.VMEM((2, 256, 256), F32),
-            pltpu.VMEM((2, 2, CA, 16, 256), BF),
-            pltpu.VMEM((2, 2, CA, 16, 256), BF),
+            pltpu.VMEM((2, 2, 2, 16, 16, 256), BF),
+            pltpu.VMEM((2, 2, 2, 16, 16, 256), BF),
             pltpu.VMEM((256, 512), BF),
             pltpu.VMEM((128, 256), BF),
             pltpu.VMEM((256, NZ), BF),
@@ -291,14 +308,14 @@
             pltpu.SemaphoreType.DMA((7,)),
             pltpu.SemaphoreType.DMA((7,)),
             pltpu.SemaphoreType.DMA((7,)),
-            pltpu.SemaphoreType.DMA((2,)),
-            pltpu.SemaphoreType.DMA((2,)),
-            pltpu.SemaphoreType.DMA((4,)),
-            pltpu.SemaphoreType.DMA((4,)),
+            pltpu.SemaphoreType.DMA((2, 8)),
+            pltpu.SemaphoreType.DMA((2, 8)),
+            pltpu.SemaphoreType.DMA((8,)),
+            pltpu.SemaphoreType.DMA((8,)),
         ],
         compiler_params=pltpu.CompilerParams(vmem_limit_bytes=40 << 20, collective_id=0, has_side_effects=True),
         name="deposit_and_smooth",
-    )(parcels[0, 0], cell_index[0, 0], counts[0], coupling)
+    )(*inputs)
 
 
 def solution(mesh):

time: 49.4 us -> 46.3 us (0.937)
  local copies, waits for them, and re-layouts: 4.36 us -> 1.32 us
    unnamed x9 -> x1, local copies, waits for them, and re-layouts: 4.36 us -> 1.32 us
where the time goes in v4:
time: 46.3 us; the launch traced here: 46.2 us
  Pallas kernels  44.9 us (97%)
  local copies, waits for them, and re-layouts  1.32 us (3%)
    pallas_call x1, Pallas kernels, on_device(): pl.pallas_call(whole_kernel, out_shape=jax.ShapeDtypeStruct((COMP, CA, CY...  44.9 us
    unnamed x1, local copies, waits for them, and re-layouts  1.32 us

profile of v4, /device:TPU:1, one launch (start us, length us, event | category | flops | bytes accessed | tf_op | source)
XLA Modules:
  0.0 46.2 jit_solution(17015979180672286283)
XLA Ops:
  0.0 44.9 %deposit_and_smooth.1 = f32[4,32,32,128]{3,2,1,0:T(8,128)S(1)} custom-call(bf16[64,16,64]{2,1,0:T(8,128)(2,1)} %bitcast.3, s32[64,64]{1,0:T(8,128)} %bitcast.4, s32[1,64]{1,0:T(1,128)} %bitcast.5, bf16[4,16]{1,0:T(4,128)(2,1)} %coupling_hbm.1), custom_call_target="tpu_custom_call" | custom-call | tf_op jit(solution)/shard_map/deposit_and_smooth/pallas_call | solution.py:279
  44.9 1.3 %copy.6 = f32[4,32,32,128]{3,2,1,0:T(8,128)} copy(f32[4,32,32,128]{3,2,1,0:T(8,128)S(1)} %deposit_and_smooth.1) | data formatting | bytes 4194304

commit v5 on v4

--- a/solution.py
+++ b/solution.py
@@ -82,7 +82,7 @@
 
 def whole_kernel(
     parcels_hbm, cell_hbm, counts_hbm, coupling_hbm, out_ref,
-    parcels_ref, cell_ref, counts_ref, coupling_ref, msg1, buf1, msg2, lists, flat, keys, wt, picks, acc_own, acc_side, e_own, e_side, kxs, kys, kzs, sx, syz, load,
+    parcels_ref, cell_ref, counts_ref, coupling_ref, msg1, buf1, msg2, lists, flat, keys, wt, picks, acc_own, axial, acc_side, e_own, e_side, kxs, kys, kzs, sx, syz, load,
     send1, recv1, send2, recv2, send_ax, recv_ax, send_cr, recv_cr,
 ):
     a, c_at = lax.axis_index("ax"), lax.axis_index("cr")
@@ -168,22 +168,21 @@
     for h in range(2):
         for i in range(4):
             msg2[4 * h + i] = jnp.concatenate([halves[m][h][i * 8 : i * 8 + 8] for m in range(4)], axis=0).astype(BF)
+    place = {j: p for p, j in enumerate((0, 1, 7, 2, 6, 3, 5, 4))}
     second = {}
     for j in (4, 3, 5, 2, 6, 1, 7):
         second[j] = remote(
-            msg2.at[lax.rem(y_at + j, 8)], lists.at[0, y_at], send2.at[j - 1], recv2.at[j - 1], in_column[j - 1]
+            msg2.at[lax.rem(y_at + j, 8)], lists.at[0, place[j]], send2.at[j - 1], recv2.at[j - 1], in_column[j - 1]
         )
         second[j].start()
-    lists[0, y_at] = msg2[y_at]
+    lists[0, 0] = msg2[y_at]
 
     def rows_iota(n, width):
         return iota((n, width), 0).astype(F32).astype(BF)
 
-    def source(j):
-        return lax.rem(y_at + 8 - j, 8)
-
-    def unfold(l, j, ks):
-        rows = lists[l, source(j)].astype(F32)
+    def unfold(l, p):
+        ks = slice(p * 512, p * 512 + 512)
+        rows = lists[l, p].astype(F32)
         flat[l, :, ks] = jnp.concatenate([rows[b * 8 : b * 8 + 8] for b in range(4)], axis=1)
         hit = jnp.broadcast_to(flat[l, 4:5, ks].astype(BF), (NZ, 512)) == rows_iota(NZ, 512)
         for f in range(COMP):
@@ -203,35 +202,48 @@
             parts.append(jnp.where(key == rows_iota(n, width), one, zero))
         return jnp.concatenate(parts, axis=0)
 
+    def deposit(first_place, last_place):
+        for p in range(first_place, last_place):
+            unfold(0, p)
+        ks = slice(first_place * 512, last_place * 512)
+        for c in range(2):
+            rows = range(c * ROWS, c * ROWS + ROWS)
+            d = lax.dot_general(
+                picked(0, rows, ks, ks.stop - ks.start), wt[0, :, ks], NT, preferred_element_type=F32
+            )
+            acc_own[c] = d if first_place == 0 else acc_own[c] + d
+
     along = {}
-    at = 0
-    order = ((0,), (1, 7), (2, 6), (3, 5), (4,))
-    for step in order:
-        for j in step:
-            if j:
-                second[j].wait_recv()
-            for k, to in ((0, up), (1, down)):
-                along[k, j] = remote(
-                    lists.at[0, source(j)], lists.at[1 + k, source(j)], send_ax.at[k, j], recv_ax.at[k, j], (to, c_at)
-                )
-                along[k, j].start()
-        for b, j in enumerate(step):
-            unfold(0, j, slice(at + b * 512, at + b * 512 + 512))
-        width = 512 * len(step)
-        ks = slice(at, at + width)
-        for c in range(2):
-            d = lax.dot_general(
-                picked(0, range(c * ROWS, c * ROWS + ROWS), ks, width), wt[0, :, ks], NT, preferred_element_type=F32
+
+    def hand_on(part, first_place, last_place):
+        ps = pl.ds(first_place, last_place - first_place)
+        for k, to in ((0, up), (1, down)):
+            along[k, part] = remote(
+                lists.at[0, ps], lists.at[1 + k, ps], send_ax.at[k, part], recv_ax.at[k, part], (to, c_at)
             )
-            acc_own[c] = d if at == 0 else acc_own[c] + d
-        at += width
-    at = 0
-    for step in order:
-        for j in step:
-            for l in (1, 2):
-                along[l - 1, j].wait_recv()
-                unfold(l, j, slice(at, at + 512))
-            at += 512
+            along[k, part].start()
+
+    deposit(0, 1)
+    for j in (1, 7):
+        second[j].wait_recv()
+    hand_on(0, 0, 3)
+    deposit(1, 3)
+    for j in (2, 6, 3, 5, 4):
+        second[j].wait_recv()
+    hand_on(1, 3, 8)
+    deposit(3, 8)
+    for h in range(2):
+        for i in range(2):
+            for c in range(2):
+                high, low = split(acc_own[c, i * 256 : i * 256 + 256, h * 256 : h * 256 + 256])
+                v = jnp.dot(kxs[:, :256], high, preferred_element_type=F32)
+                v += jnp.dot(kxs[:, :256], low, preferred_element_type=F32)
+                axial[h, i, c] = v
+    for part, places in enumerate((range(3), range(3, 8))):
+        for l in (1, 2):
+            along[l - 1, part].wait_recv()
+            for p in places:
+                unfold(l, p)
     across = []
     for h in range(2):
         fs = slice(h * 256, h * 256 + 256)
@@ -242,11 +254,11 @@
                     picks[i, l - 1] = picked(l, rows, slice(0, SLOTS), SLOTS)
                 acc_side[l - 1] = lax.dot_general(picks[i, l - 1], wt[l, fs, :], NT, preferred_element_type=F32)
             for c in range(2):
-                own = acc_own[c, i * 256 : i * 256 + 256, fs]
                 sides = [acc_side[k, c * 128 : c * 128 + 128, :] for k in range(2)]
-                high, low = split(jnp.concatenate([own] + sides, axis=0))
-                v = jnp.dot(kxs[...], high, preferred_element_type=F32)
-                v += jnp.dot(kxs[...], low, preferred_element_type=F32)
+                high, low = split(jnp.concatenate(sides, axis=0))
+                v = jnp.dot(kxs[:, 256:], high, preferred_element_type=F32)
+                v += jnp.dot(kxs[:, 256:], low, preferred_element_type=F32)
+                v += axial[h, i, c]
                 e_own[h, i, c] = v.astype(BF).reshape(16, 16, 256)
                 k = h * 4 + i * 2 + c
                 across.append(
@@ -295,6 +307,7 @@
             pltpu.VMEM((3, FZ, SLOTS), BF),
             pltpu.VMEM((2, 2, 256, SLOTS), BF),
             pltpu.VMEM((2, 512, FZ), F32),
+            pltpu.VMEM((2, 2, 2, 256, 256), F32),
             pltpu.VMEM((2, 256, 256), F32),
             pltpu.VMEM((2, 2, 2, 16, 16, 256), BF),
             pltpu.VMEM((2, 2, 2, 16, 16, 256), BF),
@@ -308,8 +321,8 @@
             pltpu.SemaphoreType.DMA((7,)),
             pltpu.SemaphoreType.DMA((7,)),
             pltpu.SemaphoreType.DMA((7,)),
-            pltpu.SemaphoreType.DMA((2, 8)),
-            pltpu.SemaphoreType.DMA((2, 8)),
+            pltpu.SemaphoreType.DMA((2, 2)),
+            pltpu.SemaphoreType.DMA((2, 2)),
             pltpu.SemaphoreType.DMA((8,)),
             pltpu.SemaphoreType.DMA((8,)),
         ],

time: 46.3 us -> 44.1 us (0.952)
  Pallas kernels: 44.9 us -> 42.6 us
    pallas_call x1, Pallas kernels: 44.9 us -> 42.6 us  [on_device(): pl.pallas_call(whole_kernel, out_shape=jax.ShapeDtypeStruct((COMP, CA, CY...]
where the time goes in v5:
time: 44.1 us; the launch traced here: 43.9 us
  Pallas kernels  42.6 us (97%)
  local copies, waits for them, and re-layouts  1.32 us (3%)
    pallas_call x1, Pallas kernels, on_device(): pl.pallas_call(whole_kernel, out_shape=jax.ShapeDtypeStruct((COMP, CA, CY...  42.6 us
    unnamed x1, local copies, waits for them, and re-layouts  1.32 us

profile of v5, /device:TPU:1, one launch (start us, length us, event | category | flops | bytes accessed | tf_op | source)
XLA Modules:
  0.0 43.9 jit_solution(10543561803913875850)
XLA Ops:
  0.0 42.6 %deposit_and_smooth.1 = f32[4,32,32,128]{3,2,1,0:T(8,128)S(1)} custom-call(bf16[64,16,64]{2,1,0:T(8,128)(2,1)} %bitcast.3, s32[64,64]{1,0:T(8,128)} %bitcast.4, s32[1,64]{1,0:T(1,128)} %bitcast.5, bf16[4,16]{1,0:T(4,128)(2,1)} %coupling_hbm.1), custom_call_target="tpu_custom_call" | custom-call | tf_op jit(solution)/shard_map/deposit_and_smooth/pallas_call | solution.py:291
  42.6 1.3 %copy.6 = f32[4,32,32,128]{3,2,1,0:T(8,128)} copy(f32[4,32,32,128]{3,2,1,0:T(8,128)S(1)} %deposit_and_smooth.1) | data formatting | bytes 4194304

commit v6 on v5

--- a/solution.py
+++ b/solution.py
@@ -244,17 +244,21 @@
             along[l - 1, part].wait_recv()
             for p in places:
                 unfold(l, p)
+    for l in (1, 2):
+        for i in range(2):
+            rows = [c * ROWS + i * 8 + k for c in range(2) for k in range(8)]
+            picks[l - 1, i * 256 : i * 256 + 256] = picked(l, rows, slice(0, SLOTS), SLOTS)
     across = []
     for h in range(2):
         fs = slice(h * 256, h * 256 + 256)
         for i in range(2):
-            for l in (1, 2):
-                if h == 0:
-                    rows = [c * ROWS + i * 8 + k for c in range(2) for k in range(8)]
-                    picks[i, l - 1] = picked(l, rows, slice(0, SLOTS), SLOTS)
-                acc_side[l - 1] = lax.dot_general(picks[i, l - 1], wt[l, fs, :], NT, preferred_element_type=F32)
+            part = slice(i * 256, i * 256 + 256) if h else slice(0, 512)
+            for l in (1, 2) if h or i == 0 else ():
+                acc_side[l - 1, part] = lax.dot_general(
+                    picks[l - 1, part], wt[l, fs, :], NT, preferred_element_type=F32
+                )
             for c in range(2):
-                sides = [acc_side[k, c * 128 : c * 128 + 128, :] for k in range(2)]
+                sides = [acc_side[k, i * 256 + c * 128 : i * 256 + c * 128 + 128, :] for k in range(2)]
                 high, low = split(jnp.concatenate(sides, axis=0))
                 v = jnp.dot(kxs[:, 256:], high, preferred_element_type=F32)
                 v += jnp.dot(kxs[:, 256:], low, preferred_element_type=F32)
@@ -268,17 +272,19 @@
     for h in range(2):
         for copy in across[4 * h : 4 * h + 4]:
             copy.wait_recv()
-        for g in range(CA // 4):
-            xs = slice(g * 2, g * 2 + 2)
-            rhs = [e[h, i, c, xs].reshape(32, 256) for e in (e_own, e_side) for c in range(2) for i in range(2)]
-            v = jnp.dot(kys[...], jnp.concatenate(rhs, axis=0), preferred_element_type=F32)
-            high, low = split(jnp.concatenate([v[:, :128], v[:, 128:]], axis=0))
-            v = jnp.dot(jnp.concatenate([high, low], axis=1), kzs[...], preferred_element_type=F32)
-            v = v.reshape(2, 4, CY, NZ)
-            for i in range(4):
-                scale = syz[...] * sx[g * 4 + i : g * 4 + i + 1, :]
-                for f in range(2):
-                    out_ref[2 * h + f, g * 4 + i] = v[f, i] * scale
+        for start in range(0, CA // 4, 8):
+            crossed = []
+            for g in range(start, start + 8):
+                xs = slice(g * 2, g * 2 + 2)
+                rhs = [e[h, i, c, xs].reshape(32, 256) for e in (e_own, e_side) for c in range(2) for i in range(2)]
+                crossed.append(jnp.dot(kys[...], jnp.concatenate(rhs, axis=0), preferred_element_type=F32))
+            for f in range(2):
+                high, low = split(jnp.concatenate([v[:, f * 128 : f * 128 + 128] for v in crossed], axis=0))
+                v = jnp.dot(jnp.concatenate([high, low], axis=1), kzs[...], preferred_element_type=F32)
+                v = v.reshape(32, CY, NZ)
+                for i in range(32):
+                    x = start * 4 + i
+                    out_ref[2 * h + f, x] = v[i] * (syz[...] * sx[x : x + 1, :])
     for copy in first + list(second.values()) + list(along.values()) + across:
         copy.wait_send()
 
@@ -305,10 +311,10 @@
             pltpu.VMEM((3, 8, SLOTS), F32),
             pltpu.VMEM((3, CY, SLOTS), F32),
             pltpu.VMEM((3, FZ, SLOTS), BF),
-            pltpu.VMEM((2, 2, 256, SLOTS), BF),
+            pltpu.VMEM((2, 512, SLOTS), BF),
             pltpu.VMEM((2, 512, FZ), F32),
             pltpu.VMEM((2, 2, 2, 256, 256), F32),
-            pltpu.VMEM((2, 256, 256), F32),
+            pltpu.VMEM((2, 512, 256), F32),
             pltpu.VMEM((2, 2, 2, 16, 16, 256), BF),
             pltpu.VMEM((2, 2, 2, 16, 16, 256), BF),
             pltpu.VMEM((256, 512), BF),

time: 44.1 us -> 44.5 us (level)
  Pallas kernels: 42.6 us -> 43.1 us
    pallas_call x1, Pallas kernels: 42.6 us -> 43.1 us  [on_device(): pl.pallas_call(whole_kernel, out_shape=jax.ShapeDtypeStruct((COMP, CA, CY...]
where the time goes in v6:
time: 44.5 us; the launch traced here: 44.4 us
  Pallas kernels  43.1 us (97%)
  local copies, waits for them, and re-layouts  1.32 us (3%)
    pallas_call x1, Pallas kernels, on_device(): pl.pallas_call(whole_kernel, out_shape=jax.ShapeDtypeStruct((COMP, CA, CY...  43.1 us
    unnamed x1, local copies, waits for them, and re-layouts  1.32 us

profile of v6, /device:TPU:1, one launch (start us, length us, event | category | flops | bytes accessed | tf_op | source)
XLA Modules:
  0.0 44.4 jit_solution(13157466647177996002)
XLA Ops:
  0.0 43.1 %deposit_and_smooth.1 = f32[4,32,32,128]{3,2,1,0:T(8,128)S(1)} custom-call(bf16[64,16,64]{2,1,0:T(8,128)(2,1)} %bitcast.3, s32[64,64]{1,0:T(8,128)} %bitcast.4, s32[1,64]{1,0:T(1,128)} %bitcast.5, bf16[4,16]{1,0:T(4,128)(2,1)} %coupling_hbm.1), custom_call_target="tpu_custom_call" | custom-call | tf_op jit(solution)/shard_map/deposit_and_smooth/pallas_call | solution.py:297
  43.1 1.3 %copy.6 = f32[4,32,32,128]{3,2,1,0:T(8,128)} copy(f32[4,32,32,128]{3,2,1,0:T(8,128)S(1)} %deposit_and_smooth.1) | data formatting | bytes 4194304

commit v7 on v6

--- a/solution.py
+++ b/solution.py
@@ -244,21 +244,17 @@
             along[l - 1, part].wait_recv()
             for p in places:
                 unfold(l, p)
-    for l in (1, 2):
-        for i in range(2):
-            rows = [c * ROWS + i * 8 + k for c in range(2) for k in range(8)]
-            picks[l - 1, i * 256 : i * 256 + 256] = picked(l, rows, slice(0, SLOTS), SLOTS)
     across = []
     for h in range(2):
         fs = slice(h * 256, h * 256 + 256)
         for i in range(2):
-            part = slice(i * 256, i * 256 + 256) if h else slice(0, 512)
-            for l in (1, 2) if h or i == 0 else ():
-                acc_side[l - 1, part] = lax.dot_general(
-                    picks[l - 1, part], wt[l, fs, :], NT, preferred_element_type=F32
-                )
+            for l in (1, 2):
+                if h == 0:
+                    rows = [c * ROWS + i * 8 + k for c in range(2) for k in range(8)]
+                    picks[i, l - 1] = picked(l, rows, slice(0, SLOTS), SLOTS)
+                acc_side[l - 1] = lax.dot_general(picks[i, l - 1], wt[l, fs, :], NT, preferred_element_type=F32)
             for c in range(2):
-                sides = [acc_side[k, i * 256 + c * 128 : i * 256 + c * 128 + 128, :] for k in range(2)]
+                sides = [acc_side[k, c * 128 : c * 128 + 128, :] for k in range(2)]
                 high, low = split(jnp.concatenate(sides, axis=0))
                 v = jnp.dot(kxs[:, 256:], high, preferred_element_type=F32)
                 v += jnp.dot(kxs[:, 256:], low, preferred_element_type=F32)
@@ -311,10 +307,10 @@
             pltpu.VMEM((3, 8, SLOTS), F32),
             pltpu.VMEM((3, CY, SLOTS), F32),
             pltpu.VMEM((3, FZ, SLOTS), BF),
-            pltpu.VMEM((2, 512, SLOTS), BF),
+            pltpu.VMEM((2, 2, 256, SLOTS), BF),
             pltpu.VMEM((2, 512, FZ), F32),
             pltpu.VMEM((2, 2, 2, 256, 256), F32),
-            pltpu.VMEM((2, 512, 256), F32),
+            pltpu.VMEM((2, 256, 256), F32),
             pltpu.VMEM((2, 2, 2, 16, 16, 256), BF),
             pltpu.VMEM((2, 2, 2, 16, 16, 256), BF),
             pltpu.VMEM((256, 512), BF),

time: 44.5 us -> 43.7 us (0.982)
  Pallas kernels: 43.1 us -> 42.2 us
    pallas_call x1, Pallas kernels: 43.1 us -> 42.2 us  [on_device(): pl.pallas_call(whole_kernel, out_shape=jax.ShapeDtypeStruct((COMP, CA, CY...]
where the time goes in v7:
time: 43.7 us; the launch traced here: 43.5 us
  Pallas kernels  42.2 us (97%)
  local copies, waits for them, and re-layouts  1.32 us (3%)
    pallas_call x1, Pallas kernels, on_device(): pl.pallas_call(whole_kernel, out_shape=jax.ShapeDtypeStruct((COMP, CA, CY...  42.2 us
    unnamed x1, local copies, waits for them, and re-layouts  1.32 us

profile of v7, /device:TPU:1, one launch (start us, length us, event | category | flops | bytes accessed | tf_op | source)
XLA Modules:
  0.0 43.5 jit_solution(3517444693303621954)
XLA Ops:
  0.0 42.2 %deposit_and_smooth.1 = f32[4,32,32,128]{3,2,1,0:T(8,128)S(1)} custom-call(bf16[64,16,64]{2,1,0:T(8,128)(2,1)} %bitcast.3, s32[64,64]{1,0:T(8,128)} %bitcast.4, s32[1,64]{1,0:T(1,128)} %bitcast.5, bf16[4,16]{1,0:T(4,128)(2,1)} %coupling_hbm.1), custom_call_target="tpu_custom_call" | custom-call | tf_op jit(solution)/shard_map/deposit_and_smooth/pallas_call | solution.py:293
  42.2 1.3 %copy.6 = f32[4,32,32,128]{3,2,1,0:T(8,128)} copy(f32[4,32,32,128]{3,2,1,0:T(8,128)S(1)} %deposit_and_smooth.1) | data formatting | bytes 4194304
